TPU v7x, 32 devices: a whole 2x2x4 slice. The times are simulated.
32 devices in a mesh: band: 4 (over z), ty: 4 (over y, core), tx: 2 (over x).
Axes of the slice: x: 2, y: 2, z: 4, core: 2. Of those that a mesh axis runs over, the one named last changes fastest.
Arguments:
- dirty: float32 [8, 1024, 512], P('band', 'ty', 'tx'), may hold values from -6 to 6
- psf: bfloat16 [8, 20, 2304], P('band'), may hold values from -4 to 4
- comp_tile: int32 [1024, 1], P(('ty', 'tx')), may hold values from 0 to 7; in each aligned block of 128 rows (0 to 127, 128 to 255, ...) at most 32 rows name the same one
- comp_offset: int32 [1024, 2], P(('ty', 'tx')), may hold values from 0 to 255
- comp_scale: int32 [1024], P(('ty', 'tx')), may hold values from 0 to 4
- comp_amp: float32 [1024, 4], P(('ty', 'tx')), may hold values from -6 to 6
- fit_weight: float32 [8, 4], P('band'), may hold values from -5 to 5
Outputs:
- residual: float32 [8, 1024, 512], P('band', 'ty', 'tx')
- taylor_fit: float32 [4, 1024, 512], P('band', 'ty', 'tx')
Inputs may be any that keep to these rules, and one draw needn't show every extreme that they name: `comp_tile`: the 128 components of one device name at most 32 components for one tile, and exactly 32 for some tile on some device.
All inputs are finite; a program needn't handle non-finite values.
Results may differ from a plain program's by a relative error of at most 0.0022.
Values may be sent and summed in bfloat16 or wider, within the bound.
No kernel may reach another device: no remote copies, remote signals or barrier semaphores. Data moves between devices by JAX's collectives and lax.ppermute only.
A program may use at most 64 MiB of HBM per device.

v0:
```python
import functools
import math
import jax
import jax.numpy as jnp
from jax import lax
from jax.experimental import pallas as pl
from jax.experimental.pallas import tpu as pltpu
from jax.sharding import PartitionSpec as P

LANES = 128
HALF = 64
U = 16
LIST = 8
F32, BF16, I32 = jnp.float32, jnp.bfloat16, jnp.int32


def vmem():
    return pl.BlockSpec(memory_space=pltpu.VMEM)


def prep_kernel(w_hbm, tile_hbm, offset_hbm, scale_hbm, amp_hbm, dirty_hbm, psf_hbm,
                feat_ref, pay_ref, keep_ref, dsend_ref, dkeep_ref, pairs,
                w_ref, tile_ref, offset_ref, scale_ref, amp_ref, dirty_ref, psf_ref, sems, *,
                me, share, shares, n_tx, n_band, lift):
    copies = [pltpu.make_async_copy(src, dst, sems.at[i]) for i, (src, dst) in enumerate((
        (psf_hbm, psf_ref), (w_hbm, w_ref), (tile_hbm, tile_ref), (offset_hbm, offset_ref),
        (scale_hbm, scale_ref), (amp_hbm, amp_ref), (dirty_hbm, dirty_ref)))]
    for copy in copies:
        copy.start()
    bands, side = dirty_ref.shape[0], dirty_ref.shape[1]
    kk, flat = psf_ref.shape[0], psf_ref.shape[2]
    chunks = flat // LANES
    taylor = amp_ref.shape[0]
    me, share = me(), share()
    part, block = kk // shares, keep_ref.shape[1]
    copies[0].wait()
    copies[1].wait()
    for c in range(chunks):
        for k in range(kk):
            top = (c * kk + k) * bands
            pairs[top:top + bands, :] = psf_ref[k, :, c * LANES:(c + 1) * LANES].astype(F32)
    weights = [[w_ref[b, me ^ step] * (lift if step % 2 else 1.0) for b in range(bands)] for step in range(n_band)]
    for c in range(chunks):
        rows = [pairs[pl.ds((c * kk + share * part) * bands + b, part, stride=bands), :] for b in range(bands)]
        for step in range(n_band):
            total = weights[step][0] * rows[0]
            for b in range(1, bands):
                total = total + weights[step][b] * rows[b]
            (pay_ref if step % 2 else keep_ref)[step // 2, c * part:(c + 1) * part, :] = total
    spare = jnp.zeros((block - part * chunks, LANES), F32)
    for step in range(n_band):
        (pay_ref if step % 2 else keep_ref)[step // 2, part * chunks:, :] = spare
    for copy in copies[2:]:
        copy.wait()
    tile = tile_ref[0:1, :]
    feat_ref[0:1, :] = ((tile // n_tx) * side + offset_ref[0:1, :]).astype(F32)
    feat_ref[1:2, :] = ((tile % n_tx) * side + offset_ref[1:2, :]).astype(F32)
    feat_ref[2:3, :] = scale_ref[0:1, :].astype(F32)
    feat_ref[3:3 + taylor, :] = amp_ref[...]
    feat_ref[3 + taylor:, :] = jnp.zeros((LIST - 3 - taylor, LANES), F32)
    for step in range(n_band):
        total = weights[step][0] * dirty_ref[0]
        for b in range(1, bands):
            total = total + weights[step][b] * dirty_ref[b]
        (dsend_ref if step % 2 else dkeep_ref)[step // 2] = total


def prep(dirty, psf, comp_tile, comp_offset, comp_scale, comp_amp, fit_weight, me, share, shares, n_tx, n_band, lift):
    bands, kk, flat = psf.shape
    side = dirty.shape[1]
    chunks = flat // LANES
    block = -(-(kk // shares) * chunks // 16) * 16
    args = (fit_weight, comp_tile.T, comp_offset.T, comp_scale[None], comp_amp.T, dirty, psf.transpose(1, 0, 2))
    return pl.pallas_call(
        functools.partial(prep_kernel, me=me, share=share, shares=shares, n_tx=n_tx, n_band=n_band, lift=lift),
        out_shape=(
            jax.ShapeDtypeStruct((LIST, LANES), F32),
            jax.ShapeDtypeStruct((n_band // 2, block, LANES), F32),
            jax.ShapeDtypeStruct((n_band // 2, block, LANES), F32),
            jax.ShapeDtypeStruct((n_band // 2, side, side), F32),
            jax.ShapeDtypeStruct((n_band // 2, side, side), F32),
            jax.ShapeDtypeStruct((bands * kk * chunks, LANES), F32),
        ),
        in_specs=[pl.BlockSpec(memory_space=pltpu.HBM)] * len(args),
        out_specs=(vmem(),) * 6,
        scratch_shapes=[pltpu.SMEM(args[0].shape, F32)] + [pltpu.VMEM(x.shape, x.dtype) for x in args[1:]] + [
            pltpu.SemaphoreType.DMA((len(args),))],
        compiler_params=pltpu.CompilerParams(vmem_limit_bytes=12 * 1024 * 1024),
    )(*[pltpu.with_memory_space_constraint(x, pltpu.HBM) for x in args])


def pick(chunk, first, dest, lane, patch):
    c, off = divmod(first, LANES)
    a = chunk(c)
    if off + patch > LANES:
        a = jnp.where(lane >= off, a, chunk(c + 1))
    turn = (dest - off) % LANES
    return pltpu.roll(a, turn, 1) if turn else a


def pack_kernel(pairs_ref, out_ref, *, patch):
    kk = out_ref.shape[0] // patch
    lane = lax.broadcasted_iota(I32, (kk, LANES), 1)

    def chunk(b, c):
        return pairs_ref[pl.ds(c * 2 * kk + b, kk, stride=2), :]

    for u in range(patch):
        two = [pick(functools.partial(chunk, b), u * patch, b * HALF, lane, patch) for b in range(2)]
        v = jnp.where(lane < HALF, two[0], two[1])
        out_ref[pl.ds(u, kk, stride=patch), :] = jnp.where(lane % HALF < patch, v, 0.0)


def pack(pairs, patch):
    return pl.pallas_call(
        functools.partial(pack_kernel, patch=patch),
        out_shape=jax.ShapeDtypeStruct((pairs.shape[0] // 2 // (patch * patch // LANES) * patch, LANES), F32),
        in_specs=[vmem()], out_specs=vmem(),
        compiler_params=pltpu.CompilerParams(vmem_limit_bytes=4 * 1024 * 1024),
    )(pairs)


def pack_fit_kernel(psi_ref, out_ref, *, patch, shares, start):
    h = patch // 2
    n, block = out_ref.shape[0] // h // shares, psi_ref.shape[0] // shares
    lane = lax.broadcasted_iota(I32, (n, LANES), 1)
    for s in range(shares):
        top = start(s) * (n * h)

        def chunk(c):
            return psi_ref[s * block + c * n:s * block + (c + 1) * n, :]

        for u in range(h):
            v = jnp.where(lane < HALF, pick(chunk, u * patch, 0, lane, patch),
                          pick(chunk, (u + h) * patch, HALF, lane, patch))
            out_ref[pl.ds(top + u, n, stride=h), :] = jnp.where(lane % HALF < patch, v, 0.0)


def pack_fit(psi, kk, patch, shares, start):
    return pl.pallas_call(
        functools.partial(pack_fit_kernel, patch=patch, shares=shares, start=start),
        out_shape=jax.ShapeDtypeStruct((kk * (patch // 2), LANES), F32),
        in_specs=[vmem()], out_specs=vmem(),
        compiler_params=pltpu.CompilerParams(vmem_limit_bytes=4 * 1024 * 1024),
    )(psi)


def list_kernel(list_ref, words_ref, amps_ref, piece_v, rank_v, *, patch, tile, taylor, origin):
    rows = tile + 2 * patch
    S = list_ref.shape[0] // LIST

    def plane(n):
        return list_ref[pl.ds(n, S, stride=LIST), :]

    r0, c0 = origin()
    rr = plane(0).astype(I32) - r0
    cc = plane(1).astype(I32) - c0
    mask = (rr > -patch) & (rr < tile) & (cc > -patch) & (cc < tile)
    mb = jnp.where(mask, 1.0, 0.0).astype(BF16)
    i0 = lax.broadcasted_iota(I32, (LANES, LANES), 0)
    i1 = lax.broadcasted_iota(I32, (LANES, LANES), 1)
    upper = jnp.where(i0 < i1, 1.0, 0.0).astype(BF16)
    ones = jnp.ones((LANES, LANES), BF16)
    s0 = lax.broadcasted_iota(I32, (S, S), 0)
    s1 = lax.broadcasted_iota(I32, (S, S), 1)
    below = jnp.where(s1 < s0, 1.0, 0.0).astype(BF16)
    before = jnp.dot(below, mb, preferred_element_type=F32).astype(BF16)
    every = jnp.dot(jnp.ones((8, S), BF16), mb, preferred_element_type=F32).astype(BF16)
    rank = jnp.dot(mb, upper, preferred_element_type=F32) + jnp.dot(before, ones, preferred_element_type=F32)
    words_ref[S:S + 8, :] = jnp.dot(every, ones, preferred_element_type=F32).astype(I32)
    rank_v[...] = jnp.where(mask, rank, -1.0).astype(I32)
    base = jnp.where(mask, ((cc + HALF) >> 6) * rows + rr + patch, 0)
    word = base + ((cc & (LANES - 1)) << 14) + (plane(2).astype(I32) << 21)
    pieces = [(word & 255).astype(F32), ((word >> 8) & 255).astype(F32), ((word >> 16) & 255).astype(F32)]
    for t in range(taylor):
        rest = plane(3 + t)
        for _ in range(3):
            pieces.append(rest.astype(BF16).astype(F32))
            rest = rest - pieces[-1]
    for n, piece in enumerate(pieces):
        piece_v[n * S:(n + 1) * S, :] = piece
    srow = lax.broadcasted_iota(I32, (S, LANES), 0)

    def spread(d, got):
        rank = rank_v[pl.ds(d, 1), :]
        hit = (rank >> 7) == srow
        onehot = jnp.where((rank & (LANES - 1)) == i0, 1.0, 0.0).astype(BF16)
        lhs = jnp.concatenate([jnp.where(hit, piece_v[pl.ds(n * S + d, 1), :], 0.0) for n in range(len(pieces))], 0)
        return got + lax.dot_general(lhs.astype(BF16), onehot, (((1,), (1,)), ((), ())), preferred_element_type=F32)

    got = jnp.zeros((len(pieces) * S, LANES), F32)
    if S <= 16:
        for d in range(S):
            got = spread(d, got)
    else:
        got = lax.fori_loop(0, S, spread, got)
    part = [got[n * S:(n + 1) * S] for n in range(len(pieces))]
    words_ref[0:S, :] = part[0].astype(I32) + (part[1].astype(I32) << 8) + (part[2].astype(I32) << 16)
    for t in range(taylor):
        amps_ref[t * S:(t + 1) * S, :] = part[3 + 3 * t] + (part[4 + 3 * t] + part[5 + 3 * t])


def overlapping(lists, origin, *, patch, tile, taylor):
    S = lists.shape[0] // LIST
    return pl.pallas_call(
        functools.partial(list_kernel, patch=patch, tile=tile, taylor=taylor, origin=origin),
        out_shape=(jax.ShapeDtypeStruct((S + 8, LANES), I32), jax.ShapeDtypeStruct((taylor * S, LANES), F32)),
        in_specs=[vmem()], out_specs=(vmem(),) * 2,
        scratch_shapes=[pltpu.VMEM(((3 + 3 * taylor) * S, LANES), F32), pltpu.VMEM((S, LANES), I32)],
        compiler_params=pltpu.CompilerParams(vmem_limit_bytes=8 * 1024 * 1024),
    )(lists)


def render_kernel(words_ref, amps_ref, g_ref, gt_ref, dirty_hbm, res_ref, tay_ref,
                  words_s, amps_s, dirty_ref, acc, acct, sems, *, patch, tile, taylor, scales):
    rows = tile + 2 * patch
    S = words_ref.shape[0] - 8
    h = patch // 2
    copies = (pltpu.make_async_copy(words_ref, words_s, sems.at[0]),
              pltpu.make_async_copy(amps_ref, amps_s, sems.at[1]),
              pltpu.make_async_copy(dirty_hbm, dirty_ref, sems.at[2]))
    for copy in copies:
        copy.start()
    for j in range(1, acc.shape[0] // rows - 1):
        acc[pl.ds(j * rows + patch, tile), :] = jnp.zeros((tile, LANES), F32)
        acct[pl.ds(j * rows + patch - h, tile + h), :] = jnp.zeros((tile + h, LANES), F32)
    for copy in copies[:2]:
        copy.wait()
    n = words_s[S, 0]
    lane_half = lax.broadcasted_iota(I32, (1, LANES), 1) & (HALF - 1)

    def gen(it, k):
        row, col = it // (LANES // U), (it % (LANES // U)) * U + k
        word = words_s[row, col]
        base, turn, width = word & 16383, (word >> 14) & (LANES - 1), word >> 21
        gb, hb = pl.multiple_of(width * patch, 8), pl.multiple_of(width * h, 8)
        p = q = None
        for t in range(taylor):
            a = amps_s[row + t * S, col]
            x = a * g_ref[pl.ds(gb + t * scales * patch, patch), :]
            y = a * gt_ref[pl.ds(hb + t * scales * h, h), :]
            p, q = (x, y) if p is None else (p + x, q + y)
        p = p.astype(BF16).astype(F32)
        return pltpu.roll(p, turn, 1), pltpu.roll(q, turn, 1), base, turn & (HALF - 1)

    def put(p, q, base, turn):
        first = lane_half >= turn
        for ref, val, high in ((acc, p, patch), (acct, q, h)):
            here, right = pl.ds(base, high), pl.ds(base + rows, high)
            ref[here, :] = ref[here, :] + jnp.where(first, val, 0.0)
            ref[right, :] = ref[right, :] + jnp.where(first, 0.0, val)

    def step(i, carry):
        for item in [gen(i, k) for k in range(U)]:
            put(*item)
        return carry

    lax.fori_loop(0, (n + U - 1) // U, step, 0)

    copies[2].wait()
    left = lax.broadcasted_iota(I32, (tile, LANES), 1) < HALF
    for c in range(tile // LANES):
        j, cols = 2 * c + 1, slice(c * LANES, (c + 1) * LANES)

        def get(ref, jj, top):
            return ref[pl.ds(jj * rows + top, tile), :]

        x, y = get(acc, j, patch), get(acc, j + 1, patch)
        res_ref[0, :, cols] = dirty_ref[0, :, cols] - jnp.where(left, x, y)
        res_ref[1, :, cols] = dirty_ref[1, :, cols] - pltpu.roll(jnp.where(left, y, x), HALF, 1)
        up = jnp.where(left, get(acct, j, patch), get(acct, j + 1, patch))
        low = pltpu.roll(jnp.where(left, get(acct, j + 1, patch - h), get(acct, j, patch - h)), HALF, 1)
        tay_ref[0, :, cols] = up + low


def render(words, amps, g, gt, dirty, *, patch, taylor, scales):
    tile = dirty.shape[1]
    rows, tiles = tile + 2 * patch, tile // HALF + 2
    return pl.pallas_call(
        functools.partial(render_kernel, patch=patch, tile=tile, taylor=taylor, scales=scales),
        out_shape=(jax.ShapeDtypeStruct(dirty.shape, F32), jax.ShapeDtypeStruct((1,) + dirty.shape[1:], F32)),
        in_specs=[vmem()] * 4 + [pl.BlockSpec(memory_space=pltpu.HBM)], out_specs=(vmem(),) * 2,
        scratch_shapes=[
            pltpu.SMEM(words.shape, I32), pltpu.SMEM(amps.shape, F32), pltpu.VMEM(dirty.shape, F32),
            pltpu.VMEM((tiles * rows, LANES), F32), pltpu.VMEM((tiles * rows, LANES), F32),
            pltpu.SemaphoreType.DMA((3,))],
        compiler_params=pltpu.CompilerParams(vmem_limit_bytes=8 * 1024 * 1024),
    )(words, amps, g, gt, pltpu.with_memory_space_constraint(dirty, pltpu.HBM))


def per_device(dirty, psf, comp_tile, comp_offset, comp_scale, comp_amp, fit_weight):
    bands, tile = dirty.shape[0], dirty.shape[1]
    patch = math.isqrt(psf.shape[2])
    taylor = comp_amp.shape[1]
    scales = psf.shape[1] // taylor
    n_ty, n_tx, n_band = lax.axis_size("ty"), lax.axis_size("tx"), lax.axis_size("band")
    lift = 2.0 ** math.floor(math.log2(65504.0 / (bands * 30.0)))
    bits = [1 << n for n in range((n_tx - 1).bit_length())]
    bits += [n_tx << n for n in range(1, (n_ty - 1).bit_length())] + [n_tx]
    shares = 2

    def share():
        return lax.axis_index("ty") % 2

    lists, psi_send, psi_keep, dirty_send, dirty_keep, pairs = prep(
        dirty, psf, comp_tile, comp_offset, comp_scale, comp_amp, fit_weight,
        lambda: lax.axis_index("band"), share, shares, n_tx, n_band, lift)

    def across(value, bit):
        got = lax.ppermute(value.astype(jnp.float16), "band", [(i, i ^ bit) for i in range(n_band)])
        return got.astype(F32) * (1.0 / lift)

    def hop(value, bit):
        return lax.ppermute(value, ("ty", "tx"), [(i, i ^ bit) for i in range(n_ty * n_tx)])

    psi = psi_keep + across(psi_send, 1)
    total = dirty_keep + across(dirty_send, 1)
    band_bits = [1 << n for n in range(1, (n_band - 1).bit_length())]
    for n, bit in enumerate(band_bits):
        cut = psi.shape[0] // 2
        got = across(psi[cut:] * lift, bit)
        psi = psi[:cut] + got
    g = pack(pairs, patch)
    for bit in bits[:-1]:
        lists = jnp.concatenate([lists, hop(lists, bit)], 0)
    cut = lists.shape[0]
    got = hop(jnp.concatenate([lists, psi[0]], 0), bits[-1])
    lists = jnp.concatenate([lists, got[:cut]], 0)
    psi = jnp.concatenate([psi[0], got[cut:]], 0)
    words, amps = overlapping(
        lists, lambda: (lax.axis_index("ty") * tile, lax.axis_index("tx") * tile),
        patch=patch, tile=tile, taylor=taylor)
    for bit in band_bits:
        cut = total.shape[0] // 2
        total = total[:cut] + across(total[cut:] * lift, bit)
    residual, model_fit = render(
        words, amps, g, pack_fit(psi, psf.shape[1], patch, shares, lambda s: share() ^ s), dirty,
        patch=patch, taylor=taylor, scales=scales)
    return residual, total - model_fit


def solution(mesh):
    return jax.shard_map(
        per_device,
        mesh=mesh,
        in_specs=(
            P("band", "ty", "tx"),
            P("band", None, None),
            P(("ty", "tx"), None),
            P(("ty", "tx"), None),
            P(("ty", "tx")),
            P(("ty", "tx"), None),
            P("band", None),
        ),
        out_specs=(P("band", "ty", "tx"), P("band", "ty", "tx")),
        check_vma=False,
    )
```

profile of v0, /device:TPU:0, one launch (start us, length us, event | category | flops | bytes accessed | tf_op | source)
XLA Modules:
  0.0 25.9 jit_solution(9817971775709817123)
XLA Ops:
  0.6 1.4 %shard_map.86 = (f32[8,128]{1,0:T(8,128)S(1)}, f32[2,192,128]{2,1,0:T(8,128)S(1)}, f32[2,192,128]{2,1,0:T(8,128)S(1)}, f32[2,256,256]{2,1,0:T(8,128)S(1)}, f32[2...) custom-call(f32[2,4]{1,0:T(2,128)} %w_hbm.1, s32[1,128]{1,0:T(1,128)} %bitcast.10, s32[2,128]{1,0:T(2,128)} %bitcast.9, ...), custom_call_target="tpu_custom_call" | custom-call | tf_op jit(solution)/shard_map/pallas_call | solution.py:74
  2.1 3.1 %collective-permute-start.2 = (f16[2,192,128]{2,1,0:T(8,128)(2,1)S(1)}, f16[2,192,128]{2,1,0:T(8,128)(2,1)S(1)}, u32[]{:S(2)}, u32[]{:S(2)}) collective-permute-start(f16[2,192,128]{2,1,0:T(8,128)(2,1)S(1)} %convert_element_type.24), channel_id=1, source_target_pairs={{0,8},{8,0},{16,24},{24,16},{1,9},{9,1},{17,25},{25,17},{2,10},{10... | collective-permute-start | bytes 294920 | tf_op jit(solution)/shard_map/ppermute | solution.py:310
  5.2 1.5 %collective-permute-start = (f32[8,128]{1,0:T(8,128)S(1)}, f32[8,128]{1,0:T(8,128)S(1)}, u32[]{:S(2)}, u32[]{:S(2)}) collective-permute-start(f32[8,128]{1,0:T(8,128)S(1)} %get-tuple-element.12), channel_id=1, source_target_pairs={{0,1},{1,0},{2,3},{3,2},{4,5},{5,4},{6,7},{7,6},{8,9},{9,8},{10,11... | collective-permute-start | bytes 12296 | tf_op jit(solution)/shard_map/ppermute | solution.py:314
  6.7 0.5 %collective-permute-start.5 = (f16[2,256,256]{2,1,0:T(8,128)(2,1)S(1)}, f16[2,256,256]{2,1,0:T(8,128)(2,1)S(1)}, u32[]{:S(2)}, u32[]{:S(2)}) collective-permute-start(f16[2,256,256]{2,1,0:T(8,128)(2,1)S(1)} %convert_element_type.28), channel_id=1, source_target_pairs={{0,8},{8,0},{16,24},{24,16},{1,9},{9,1},{17,25},{25,17},{2,10},{10... | collective-permute-start | bytes 786440 | tf_op jit(solution)/shard_map/ppermute | solution.py:310
  7.2 0.4 %shard_map.88.g_ref = f32[960,128]{1,0:T(8,128)S(1)} custom-call(f32[720,128]{1,0:T(8,128)S(1)} %get-tuple-element.17.pairs_ref), custom_call_target="tpu_custom_call" | custom-call | tf_op jit(solution)/shard_map/pallas_call | solution.py:115
  7.6 0.5 %collective-permute-done.2 = f16[2,192,128]{2,1,0:T(8,128)(2,1)S(1)} collective-permute-done((f16[2,192,128]{2,1,0:T(8,128)(2,1)S(1)}, f16[2,192,128]{2,1,0:T(8,128)(2,1)S(1)}, u32[]{:S(2)}, u32[]{:S(2)}) %collective-permute-start.2) | collective-permute-done | bytes 98336 | tf_op jit(solution)/shard_map/ppermute | solution.py:310
  8.1 2.8 %collective-permute-start.3 = (f16[1,192,128]{2,1,0:T(8,128)(2,1)S(1)}, f16[1,192,128]{2,1,0:T(8,128)(2,1)S(1)}, u32[]{:S(2)}, u32[]{:S(2)}) collective-permute-start(f16[1,192,128]{2,1,0:T(8,128)(2,1)S(1)} %fusion.2), channel_id=1, source_target_pairs={{0,16},{8,24},{16,0},{24,8},{1,17},{9,25},{17,1},{25,9},{2,18},{10... | collective-permute-start | bytes 147464 | tf_op jit(solution)/shard_map/ppermute | solution.py:310
  10.9 0.0 collective-permute-done
  10.9 1.5 %collective-permute-start.1 = (f32[16,128]{1,0:T(8,128)S(1)}, f32[16,128]{1,0:T(8,128)S(1)}, u32[]{:S(2)}, u32[]{:S(2)}) collective-permute-start(f32[16,128]{1,0:T(8,128)S(1)} %pad_maximum_fusion.3), channel_id=1, source_target_pairs={{0,4},{1,5},{2,6},{3,7},{4,0},{5,1},{6,2},{7,3},{8,12},{9,13},{10,... | collective-permute-start | bytes 24584 | tf_op jit(solution)/shard_map/ppermute | solution.py:314
  12.4 1.5 %collective-permute-done.3 = f16[1,192,128]{2,1,0:T(8,128)(2,1)S(1)} collective-permute-done((f16[1,192,128]{2,1,0:T(8,128)(2,1)S(1)}, f16[1,192,128]{2,1,0:T(8,128)(2,1)S(1)}, u32[]{:S(2)}, u32[]{:S(2)}) %collective-permute-start.3) | collective-permute-done | bytes 49184 | tf_op jit(solution)/shard_map/ppermute | solution.py:310
  14.0 0.6 %collective-permute-done.1 = f32[16,128]{1,0:T(8,128)S(1)} collective-permute-done((f32[16,128]{1,0:T(8,128)S(1)}, f32[16,128]{1,0:T(8,128)S(1)}, u32[]{:S(2)}, u32[]{:S(2)}) %collective-permute-start.1) | collective-permute-done | bytes 8224 | tf_op jit(solution)/shard_map/ppermute | solution.py:314
  14.6 0.1 collective-permute-start.4
  14.7 0.6 %collective-permute-done.5 = f16[2,256,256]{2,1,0:T(8,128)(2,1)S(1)} collective-permute-done((f16[2,256,256]{2,1,0:T(8,128)(2,1)S(1)}, f16[2,256,256]{2,1,0:T(8,128)(2,1)S(1)}, u32[]{:S(2)}, u32[]{:S(2)}) %collective-permute-start.5) | collective-permute-done | bytes 262176 | tf_op jit(solution)/shard_map/ppermute | solution.py:310
  15.3 0.1 multiply_add_fusion
  15.4 2.3 %collective-permute-start.6 = (f16[1,256,256]{2,1,0:T(8,128)(2,1)S(1)}, f16[1,256,256]{2,1,0:T(8,128)(2,1)S(1)}, u32[]{:S(2)}, u32[]{:S(2)}) collective-permute-start(f16[1,256,256]{2,1,0:T(8,128)(2,1)S(1)} %fusion), channel_id=1, source_target_pairs={{0,16},{8,24},{16,0},{24,8},{1,17},{9,25},{17,1},{25,9},{2,18},{10... | collective-permute-start | bytes 393224 | tf_op jit(solution)/shard_map/ppermute | solution.py:310
  17.7 0.0 collective-permute-done.4
  17.7 0.6 %shard_map.87 = (s32[16,128]{1,0:T(8,128)S(1)}, f32[32,128]{1,0:T(8,128)S(1)}) custom-call(f32[64,128]{1,0:T(8,128)S(1)} %pad_maximum_fusion.2.list_ref), custom_call_target="tpu_custom_call" | custom-call | tf_op jit(solution)/shard_map/pallas_call | solution.py:205
  18.3 0.2 shard_map.89.gt_ref
  18.6 6.5 %shard_map.90 = (f32[2,256,256]{2,1,0:T(8,128)}, f32[1,256,256]{2,1,0:T(8,128)S(1)}) custom-call(s32[16,128]{1,0:T(8,128)S(1)} %get-tuple-element.15.words_ref, f32[32,128]{1,0:T(8,128)S(1)} %get-tuple-element.16.amps_ref, f32[960,128]{1,0:T(8,128)S(1)} %shard_map.88.g_ref, f32[480,128]{1,0:T(8,128)S(1)} %shard_map.89.gt_ref, f32[2,256,256]{2,1,0:T(8,128)} %dirty_hbm.3), custom_call_target="tpu_custom_call" | custom-call | tf_op jit(solution)/shard_map/pallas_call | solution.py:279
  25.1 0.0 collective-permute-done.6
  25.1 0.7 %fusion.1 = f32[1,256,256]{2,1,0:T(8,128)} fusion(f32[1,256,256]{2,1,0:T(8,128)S(1)} %get-tuple-element.21, f32[2,256,256]{2,1,0:T(8,128)S(1)} %multiply_add_fusion, f16[1,256,256]{2,1,0:T(8,128)(2,1)S(1)} %collective-permute-done.6), kind=kLoop, calls=%fused_computation.4 | loop fusion | flops 262144 | bytes 917504 | tf_op jit(solution)/shard_map/sub | solution.py:339
  (12 shorter events, 0.2 us)
Async XLA Ops:
  2.1 6.0 %collective-permute-start.2 = (f16[2,192,128]{2,1,0:T(8,128)(2,1)S(1)}, f16[2,192,128]{2,1,0:T(8,128)(2,1)S(1)}, u32[]{:S(2)}, u32[]{:S(2)}) collective-permute-start(f16[2,192,128]{2,1,0:T(8,128)(2,1)S(1)} %convert_element_type.24), channel_id=1, source_target_pairs={{0,8},{8,0},{16,24},{24,16},{1,9},{9,1},{17,25},{25,17},{2,10},{10... | collective-permute-start | bytes 294920 | tf_op jit(solution)/shard_map/ppermute | solution.py:310
  5.2 5.8 %collective-permute-start = (f32[8,128]{1,0:T(8,128)S(1)}, f32[8,128]{1,0:T(8,128)S(1)}, u32[]{:S(2)}, u32[]{:S(2)}) collective-permute-start(f32[8,128]{1,0:T(8,128)S(1)} %get-tuple-element.12), channel_id=1, source_target_pairs={{0,1},{1,0},{2,3},{3,2},{4,5},{5,4},{6,7},{7,6},{8,9},{9,8},{10,11... | collective-permute-start | bytes 12296 | tf_op jit(solution)/shard_map/ppermute | solution.py:314
  6.7 8.6 %collective-permute-start.5 = (f16[2,256,256]{2,1,0:T(8,128)(2,1)S(1)}, f16[2,256,256]{2,1,0:T(8,128)(2,1)S(1)}, u32[]{:S(2)}, u32[]{:S(2)}) collective-permute-start(f16[2,256,256]{2,1,0:T(8,128)(2,1)S(1)} %convert_element_type.28), channel_id=1, source_target_pairs={{0,8},{8,0},{16,24},{24,16},{1,9},{9,1},{17,25},{25,17},{2,10},{10... | collective-permute-start | bytes 786440 | tf_op jit(solution)/shard_map/ppermute | solution.py:310
  8.1 5.8 %collective-permute-start.3 = (f16[1,192,128]{2,1,0:T(8,128)(2,1)S(1)}, f16[1,192,128]{2,1,0:T(8,128)(2,1)S(1)}, u32[]{:S(2)}, u32[]{:S(2)}) collective-permute-start(f16[1,192,128]{2,1,0:T(8,128)(2,1)S(1)} %fusion.2), channel_id=1, source_target_pairs={{0,16},{8,24},{16,0},{24,8},{1,17},{9,25},{17,1},{25,9},{2,18},{10... | collective-permute-start | bytes 147464 | tf_op jit(solution)/shard_map/ppermute | solution.py:310
  10.9 3.7 %collective-permute-start.1 = (f32[16,128]{1,0:T(8,128)S(1)}, f32[16,128]{1,0:T(8,128)S(1)}, u32[]{:S(2)}, u32[]{:S(2)}) collective-permute-start(f32[16,128]{1,0:T(8,128)S(1)} %pad_maximum_fusion.3), channel_id=1, source_target_pairs={{0,4},{1,5},{2,6},{3,7},{4,0},{5,1},{6,2},{7,3},{8,12},{9,13},{10,... | collective-permute-start | bytes 24584 | tf_op jit(solution)/shard_map/ppermute | solution.py:314
  14.6 3.1 %collective-permute-start.4 = (f32[224,128]{1,0:T(8,128)S(1)}, f32[224,128]{1,0:T(8,128)S(1)}, u32[]{:S(2)}, u32[]{:S(2)}) collective-permute-start(f32[224,128]{1,0:T(8,128)S(1)} %pad_maximum_fusion.1), channel_id=1, source_target_pairs={{0,2},{1,3},{2,0},{3,1},{4,6},{5,7},{6,4},{7,5},{8,10},{9,11},{10,... | collective-permute-start | bytes 344072 | tf_op jit(solution)/shard_map/ppermute | solution.py:314
  15.4 9.7 %collective-permute-start.6 = (f16[1,256,256]{2,1,0:T(8,128)(2,1)S(1)}, f16[1,256,256]{2,1,0:T(8,128)(2,1)S(1)}, u32[]{:S(2)}, u32[]{:S(2)}) collective-permute-start(f16[1,256,256]{2,1,0:T(8,128)(2,1)S(1)} %fusion), channel_id=1, source_target_pairs={{0,16},{8,24},{16,0},{24,8},{1,17},{9,25},{17,1},{25,9},{2,18},{10... | collective-permute-start | bytes 393224 | tf_op jit(solution)/shard_map/ppermute | solution.py:310
where the time goes:
time: 26.1 us; the launch traced here: 25.9 us
  starting transfers between devices  11.7 us (45%)
  Pallas kernels  9.15 us (35%)
  waiting for transfers between devices  3.26 us (12%)
  other arithmetic  0.99 us (4%)
  between operations  0.74 us (3%)
    ppermute x4, starting transfers between devices, across(): lax.ppermute(value.astype(jnp.float16), 'band', [(i, i ^ bit) for i in ra...  8.62 us
    pallas_call x1, Pallas kernels, render(): pl.pallas_call(functools.partial(render_kernel, patch=patch, tile=tile, t...  6.52 us
    ppermute x3, starting transfers between devices, hop(): lax.ppermute(value, ('ty', 'tx'), [(i, i ^ bit) for i in range(n_ty * n_t...  3.08 us
    ppermute x4, waiting for transfers between devices, across(): lax.ppermute(value.astype(jnp.float16), 'band', [(i, i ^ bit) for i in ra...  2.67 us
    pallas_call x1, Pallas kernels, prep(): pl.pallas_call(functools.partial(prep_kernel, me=me, share=share, shares=...  1.41 us
    sub x1, other arithmetic, per_device(): return (residual, total - model_fit)  0.75 us
    pallas_call x1, Pallas kernels, overlapping(): pl.pallas_call(functools.partial(list_kernel, patch=patch, tile=tile, tay...  0.61 us
    ppermute x3, waiting for transfers between devices, hop(): lax.ppermute(value, ('ty', 'tx'), [(i, i ^ bit) for i in range(n_ty * n_t...  0.59 us
  transfers between devices with their start and end apart: 7, of which 4 were waited for; matrix products, arithmetic and copies ran while one was open for 1% of the time, Pallas kernels for 30%

commit v1 on v0

--- a/solution.py
+++ b/solution.py
@@ -288,6 +288,26 @@
     )(words, amps, g, gt, pltpu.with_memory_space_constraint(dirty, pltpu.HBM))
 
 
+def finish_kernel(res_ref, total_ref, fit_ref, res_hbm, tay_hbm, tay_ref, sems):
+    res = pltpu.make_async_copy(res_ref, res_hbm, sems.at[0])
+    res.start()
+    tay_ref[...] = total_ref[...] - fit_ref[...]
+    tay = pltpu.make_async_copy(tay_ref, tay_hbm, sems.at[1])
+    tay.start()
+    res.wait()
+    tay.wait()
+
+
+def finish(residual, total, model_fit):
+    return pl.pallas_call(
+        finish_kernel,
+        out_shape=(jax.ShapeDtypeStruct(residual.shape, F32), jax.ShapeDtypeStruct(total.shape, F32)),
+        in_specs=[vmem()] * 3, out_specs=(pl.BlockSpec(memory_space=pltpu.HBM),) * 2,
+        scratch_shapes=[pltpu.VMEM(total.shape, F32), pltpu.SemaphoreType.DMA((2,))],
+        compiler_params=pltpu.CompilerParams(vmem_limit_bytes=4 * 1024 * 1024),
+    )(residual, total, model_fit)
+
+
 def per_device(dirty, psf, comp_tile, comp_offset, comp_scale, comp_amp, fit_weight):
     bands, tile = dirty.shape[0], dirty.shape[1]
     patch = math.isqrt(psf.shape[2])
@@ -336,7 +356,7 @@
     residual, model_fit = render(
         words, amps, g, pack_fit(psi, psf.shape[1], patch, shares, lambda s: share() ^ s), dirty,
         patch=patch, taylor=taylor, scales=scales)
-    return residual, total - model_fit
+    return finish(residual, total, model_fit)
 
 
 def solution(mesh):

time: 26.1 us -> 25.7 us (0.985)
  waiting for transfers between devices: 3.26 us -> 6.1 us
  Pallas kernels: 9.15 us -> 6.72 us
  other arithmetic: 0.99 us -> 0.28 us
    pallas_call x1, Pallas kernels: 6.52 us -> 3.2 us  [render(): pl.pallas_call(functools.partial(render_kernel, patch=patch, tile=tile, t...]
    ppermute x4, waiting for transfers between devices: 2.67 us -> 5.51 us  [across(): lax.ppermute(value.astype(jnp.float16), 'band', [(i, i ^ bit) for i in ra...]
    pallas_call x0 -> x1, Pallas kernels: none -> 0.9 us  [finish(): pl.pallas_call(finish_kernel, out_shape=(jax.ShapeDtypeStruct(residual.sh...]
    sub x1 -> x0, other arithmetic: 0.75 us -> none  [per_device(): return (residual, total - model_fit)]
  transfers between devices with their start and end apart: 7 -> 7, of which waited for: 4 -> 5; matrix products, arithmetic and copies ran while one was open for 1% -> 1% of each run, Pallas kernels for 30% -> 17%
where the time goes in v1:
time: 25.7 us; the launch traced here: 25.6 us
  starting transfers between devices  11.7 us (46%)
  Pallas kernels  6.72 us (26%)
  waiting for transfers between devices  6.1 us (24%)
  between operations  0.74 us (3%)
  other arithmetic  0.28 us (1%)
    ppermute x4, starting transfers between devices, across(): lax.ppermute(value.astype(jnp.float16), 'band', [(i, i ^ bit) for i in ra...  8.62 us
    ppermute x4, waiting for transfers between devices, across(): lax.ppermute(value.astype(jnp.float16), 'band', [(i, i ^ bit) for i in ra...  5.51 us
    pallas_call x1, Pallas kernels, render(): pl.pallas_call(functools.partial(render_kernel, patch=patch, tile=tile, t...  3.2 us
    ppermute x3, starting transfers between devices, hop(): lax.ppermute(value, ('ty', 'tx'), [(i, i ^ bit) for i in range(n_ty * n_t...  3.08 us
    pallas_call x1, Pallas kernels, prep(): pl.pallas_call(functools.partial(prep_kernel, me=me, share=share, shares=...  1.41 us
    pallas_call x1, Pallas kernels, finish(): pl.pallas_call(finish_kernel, out_shape=(jax.ShapeDtypeStruct(residual.sh...  0.9 us
    pallas_call x1, Pallas kernels, overlapping(): pl.pallas_call(functools.partial(list_kernel, patch=patch, tile=tile, tay...  0.61 us
    ppermute x3, waiting for transfers between devices, hop(): lax.ppermute(value, ('ty', 'tx'), [(i, i ^ bit) for i in range(n_ty * n_t...  0.59 us
  transfers between devices with their start and end apart: 7, of which 5 were waited for; matrix products, arithmetic and copies ran while one was open for 1% of the time, Pallas kernels for 17%

profile of v1, /device:TPU:0, one launch (start us, length us, event | category | flops | bytes accessed | tf_op | source)
XLA Modules:
  0.0 25.6 jit_solution(3612592772083450938)
XLA Ops:
  0.6 1.4 %shard_map.86 = (f32[8,128]{1,0:T(8,128)S(1)}, f32[2,192,128]{2,1,0:T(8,128)S(1)}, f32[2,192,128]{2,1,0:T(8,128)S(1)}, f32[2,256,256]{2,1,0:T(8,128)S(1)}, f32[2...) custom-call(f32[2,4]{1,0:T(2,128)} %w_hbm.1, s32[1,128]{1,0:T(1,128)} %bitcast.10, s32[2,128]{1,0:T(2,128)} %bitcast.9, ...), custom_call_target="tpu_custom_call" | custom-call | tf_op jit(solution)/shard_map/pallas_call | solution.py:74
  2.1 3.1 %collective-permute-start.2 = (f16[2,192,128]{2,1,0:T(8,128)(2,1)S(1)}, f16[2,192,128]{2,1,0:T(8,128)(2,1)S(1)}, u32[]{:S(2)}, u32[]{:S(2)}) collective-permute-start(f16[2,192,128]{2,1,0:T(8,128)(2,1)S(1)} %convert_element_type.24), channel_id=1, source_target_pairs={{0,8},{8,0},{16,24},{24,16},{1,9},{9,1},{17,25},{25,17},{2,10},{10... | collective-permute-start | bytes 294920 | tf_op jit(solution)/shard_map/ppermute | solution.py:330
  5.2 1.5 %collective-permute-start = (f32[8,128]{1,0:T(8,128)S(1)}, f32[8,128]{1,0:T(8,128)S(1)}, u32[]{:S(2)}, u32[]{:S(2)}) collective-permute-start(f32[8,128]{1,0:T(8,128)S(1)} %get-tuple-element.12), channel_id=1, source_target_pairs={{0,1},{1,0},{2,3},{3,2},{4,5},{5,4},{6,7},{7,6},{8,9},{9,8},{10,11... | collective-permute-start | bytes 12296 | tf_op jit(solution)/shard_map/ppermute | solution.py:334
  6.7 0.5 %collective-permute-start.5 = (f16[2,256,256]{2,1,0:T(8,128)(2,1)S(1)}, f16[2,256,256]{2,1,0:T(8,128)(2,1)S(1)}, u32[]{:S(2)}, u32[]{:S(2)}) collective-permute-start(f16[2,256,256]{2,1,0:T(8,128)(2,1)S(1)} %convert_element_type.28), channel_id=1, source_target_pairs={{0,8},{8,0},{16,24},{24,16},{1,9},{9,1},{17,25},{25,17},{2,10},{10... | collective-permute-start | bytes 786440 | tf_op jit(solution)/shard_map/ppermute | solution.py:330
  7.2 0.4 %shard_map.88.g_ref = f32[960,128]{1,0:T(8,128)S(1)} custom-call(f32[720,128]{1,0:T(8,128)S(1)} %get-tuple-element.17.pairs_ref), custom_call_target="tpu_custom_call" | custom-call | tf_op jit(solution)/shard_map/pallas_call | solution.py:115
  7.6 0.5 %collective-permute-done.2 = f16[2,192,128]{2,1,0:T(8,128)(2,1)S(1)} collective-permute-done((f16[2,192,128]{2,1,0:T(8,128)(2,1)S(1)}, f16[2,192,128]{2,1,0:T(8,128)(2,1)S(1)}, u32[]{:S(2)}, u32[]{:S(2)}) %collective-permute-start.2) | collective-permute-done | bytes 98336 | tf_op jit(solution)/shard_map/ppermute | solution.py:330
  8.1 2.8 %collective-permute-start.3 = (f16[1,192,128]{2,1,0:T(8,128)(2,1)S(1)}, f16[1,192,128]{2,1,0:T(8,128)(2,1)S(1)}, u32[]{:S(2)}, u32[]{:S(2)}) collective-permute-start(f16[1,192,128]{2,1,0:T(8,128)(2,1)S(1)} %fusion.1), channel_id=1, source_target_pairs={{0,16},{8,24},{16,0},{24,8},{1,17},{9,25},{17,1},{25,9},{2,18},{10... | collective-permute-start | bytes 147464 | tf_op jit(solution)/shard_map/ppermute | solution.py:330
  10.9 0.0 collective-permute-done
  10.9 1.5 %collective-permute-start.1 = (f32[16,128]{1,0:T(8,128)S(1)}, f32[16,128]{1,0:T(8,128)S(1)}, u32[]{:S(2)}, u32[]{:S(2)}) collective-permute-start(f32[16,128]{1,0:T(8,128)S(1)} %pad_maximum_fusion.3), channel_id=1, source_target_pairs={{0,4},{1,5},{2,6},{3,7},{4,0},{5,1},{6,2},{7,3},{8,12},{9,13},{10,... | collective-permute-start | bytes 24584 | tf_op jit(solution)/shard_map/ppermute | solution.py:334
  12.4 1.5 %collective-permute-done.3 = f16[1,192,128]{2,1,0:T(8,128)(2,1)S(1)} collective-permute-done((f16[1,192,128]{2,1,0:T(8,128)(2,1)S(1)}, f16[1,192,128]{2,1,0:T(8,128)(2,1)S(1)}, u32[]{:S(2)}, u32[]{:S(2)}) %collective-permute-start.3) | collective-permute-done | bytes 49184 | tf_op jit(solution)/shard_map/ppermute | solution.py:330
  14.0 0.6 %collective-permute-done.1 = f32[16,128]{1,0:T(8,128)S(1)} collective-permute-done((f32[16,128]{1,0:T(8,128)S(1)}, f32[16,128]{1,0:T(8,128)S(1)}, u32[]{:S(2)}, u32[]{:S(2)}) %collective-permute-start.1) | collective-permute-done | bytes 8224 | tf_op jit(solution)/shard_map/ppermute | solution.py:334
  14.6 0.1 collective-permute-start.4
  14.7 0.6 %collective-permute-done.5 = f16[2,256,256]{2,1,0:T(8,128)(2,1)S(1)} collective-permute-done((f16[2,256,256]{2,1,0:T(8,128)(2,1)S(1)}, f16[2,256,256]{2,1,0:T(8,128)(2,1)S(1)}, u32[]{:S(2)}, u32[]{:S(2)}) %collective-permute-start.5) | collective-permute-done | bytes 262176 | tf_op jit(solution)/shard_map/ppermute | solution.py:330
  15.3 0.1 multiply_add_fusion
  15.4 2.3 %collective-permute-start.6 = (f16[1,256,256]{2,1,0:T(8,128)(2,1)S(1)}, f16[1,256,256]{2,1,0:T(8,128)(2,1)S(1)}, u32[]{:S(2)}, u32[]{:S(2)}) collective-permute-start(f16[1,256,256]{2,1,0:T(8,128)(2,1)S(1)} %fusion), channel_id=1, source_target_pairs={{0,16},{8,24},{16,0},{24,8},{1,17},{9,25},{17,1},{25,9},{2,18},{10... | collective-permute-start | bytes 393224 | tf_op jit(solution)/shard_map/ppermute | solution.py:330
  17.7 0.0 collective-permute-done.4
  17.7 0.6 %shard_map.87 = (s32[16,128]{1,0:T(8,128)S(1)}, f32[32,128]{1,0:T(8,128)S(1)}) custom-call(f32[64,128]{1,0:T(8,128)S(1)} %pad_maximum_fusion.2.list_ref), custom_call_target="tpu_custom_call" | custom-call | tf_op jit(solution)/shard_map/pallas_call | solution.py:205
  18.3 0.2 shard_map.89.gt_ref
  18.6 3.2 %shard_map.90 = (f32[2,256,256]{2,1,0:T(8,128)S(1)}, f32[1,256,256]{2,1,0:T(8,128)S(1)}) custom-call(s32[16,128]{1,0:T(8,128)S(1)} %get-tuple-element.15.words_ref, f32[32,128]{1,0:T(8,128)S(1)} %get-tuple-element.16.amps_ref, f32[960,128]{1,0:T(8,128)S(1)} %shard_map.88.g_ref, f32[480,128]{1,0:T(8,128)S(1)} %shard_map.89.gt_ref, f32[2,256,256]{2,1,0:T(8,128)} %dirty_hbm.3), custom_call_target="tpu_custom_call" | custom-call | tf_op jit(solution)/shard_map/pallas_call | solution.py:279
  21.8 2.8 %collective-permute-done.6 = f16[1,256,256]{2,1,0:T(8,128)(2,1)S(1)} collective-permute-done((f16[1,256,256]{2,1,0:T(8,128)(2,1)S(1)}, f16[1,256,256]{2,1,0:T(8,128)(2,1)S(1)}, u32[]{:S(2)}, u32[]{:S(2)}) %collective-permute-start.6) | collective-permute-done | bytes 131104 | tf_op jit(solution)/shard_map/ppermute | solution.py:330
  24.7 0.9 %shard_map.91 = (f32[2,256,256]{2,1,0:T(8,128)}, f32[1,256,256]{2,1,0:T(8,128)}) custom-call(f32[2,256,256]{2,1,0:T(8,128)S(1)} %get-tuple-element.18.res_ref, f32[1,256,256]{2,1,0:T(8,128)S(1)} %slice_add_fusion.total_ref, f32[1,256,256]{2,1,0:T(8,128)S(1)} %get-tuple-element.21.fit_ref), custom_call_target="tpu_custom_call" | custom-call | tf_op jit(solution)/shard_map/pallas_call | solution.py:302
  (13 shorter events, 0.2 us)
Async XLA Ops:
  2.1 6.0 %collective-permute-start.2 = (f16[2,192,128]{2,1,0:T(8,128)(2,1)S(1)}, f16[2,192,128]{2,1,0:T(8,128)(2,1)S(1)}, u32[]{:S(2)}, u32[]{:S(2)}) collective-permute-start(f16[2,192,128]{2,1,0:T(8,128)(2,1)S(1)} %convert_element_type.24), channel_id=1, source_target_pairs={{0,8},{8,0},{16,24},{24,16},{1,9},{9,1},{17,25},{25,17},{2,10},{10... | collective-permute-start | bytes 294920 | tf_op jit(solution)/shard_map/ppermute | solution.py:330
  5.2 5.8 %collective-permute-start = (f32[8,128]{1,0:T(8,128)S(1)}, f32[8,128]{1,0:T(8,128)S(1)}, u32[]{:S(2)}, u32[]{:S(2)}) collective-permute-start(f32[8,128]{1,0:T(8,128)S(1)} %get-tuple-element.12), channel_id=1, source_target_pairs={{0,1},{1,0},{2,3},{3,2},{4,5},{5,4},{6,7},{7,6},{8,9},{9,8},{10,11... | collective-permute-start | bytes 12296 | tf_op jit(solution)/shard_map/ppermute | solution.py:334
  6.7 8.6 %collective-permute-start.5 = (f16[2,256,256]{2,1,0:T(8,128)(2,1)S(1)}, f16[2,256,256]{2,1,0:T(8,128)(2,1)S(1)}, u32[]{:S(2)}, u32[]{:S(2)}) collective-permute-start(f16[2,256,256]{2,1,0:T(8,128)(2,1)S(1)} %convert_element_type.28), channel_id=1, source_target_pairs={{0,8},{8,0},{16,24},{24,16},{1,9},{9,1},{17,25},{25,17},{2,10},{10... | collective-permute-start | bytes 786440 | tf_op jit(solution)/shard_map/ppermute | solution.py:330
  8.1 5.8 %collective-permute-start.3 = (f16[1,192,128]{2,1,0:T(8,128)(2,1)S(1)}, f16[1,192,128]{2,1,0:T(8,128)(2,1)S(1)}, u32[]{:S(2)}, u32[]{:S(2)}) collective-permute-start(f16[1,192,128]{2,1,0:T(8,128)(2,1)S(1)} %fusion.1), channel_id=1, source_target_pairs={{0,16},{8,24},{16,0},{24,8},{1,17},{9,25},{17,1},{25,9},{2,18},{10... | collective-permute-start | bytes 147464 | tf_op jit(solution)/shard_map/ppermute | solution.py:330
  10.9 3.7 %collective-permute-start.1 = (f32[16,128]{1,0:T(8,128)S(1)}, f32[16,128]{1,0:T(8,128)S(1)}, u32[]{:S(2)}, u32[]{:S(2)}) collective-permute-start(f32[16,128]{1,0:T(8,128)S(1)} %pad_maximum_fusion.3), channel_id=1, source_target_pairs={{0,4},{1,5},{2,6},{3,7},{4,0},{5,1},{6,2},{7,3},{8,12},{9,13},{10,... | collective-permute-start | bytes 24584 | tf_op jit(solution)/shard_map/ppermute | solution.py:334
  14.6 3.1 %collective-permute-start.4 = (f32[224,128]{1,0:T(8,128)S(1)}, f32[224,128]{1,0:T(8,128)S(1)}, u32[]{:S(2)}, u32[]{:S(2)}) collective-permute-start(f32[224,128]{1,0:T(8,128)S(1)} %pad_maximum_fusion.1), channel_id=1, source_target_pairs={{0,2},{1,3},{2,0},{3,1},{4,6},{5,7},{6,4},{7,5},{8,10},{9,11},{10,... | collective-permute-start | bytes 344072 | tf_op jit(solution)/shard_map/ppermute | solution.py:334
  15.4 9.2 %collective-permute-start.6 = (f16[1,256,256]{2,1,0:T(8,128)(2,1)S(1)}, f16[1,256,256]{2,1,0:T(8,128)(2,1)S(1)}, u32[]{:S(2)}, u32[]{:S(2)}) collective-permute-start(f16[1,256,256]{2,1,0:T(8,128)(2,1)S(1)} %fusion), channel_id=1, source_target_pairs={{0,16},{8,24},{16,0},{24,8},{1,17},{9,25},{17,1},{25,9},{2,18},{10... | collective-permute-start | bytes 393224 | tf_op jit(solution)/shard_map/ppermute | solution.py:330

commit v2 on v1

--- a/solution.py
+++ b/solution.py
@@ -120,7 +120,7 @@
     )(pairs)
 
 
-def pack_fit_kernel(psi_ref, out_ref, *, patch, shares, start):
+def pack_fit(psi_ref, out_ref, *, patch, shares, start):
     h = patch // 2
     n, block = out_ref.shape[0] // h // shares, psi_ref.shape[0] // shares
     lane = lax.broadcasted_iota(I32, (n, LANES), 1)
@@ -136,16 +136,7 @@
             out_ref[pl.ds(top + u, n, stride=h), :] = jnp.where(lane % HALF < patch, v, 0.0)
 
 
-def pack_fit(psi, kk, patch, shares, start):
-    return pl.pallas_call(
-        functools.partial(pack_fit_kernel, patch=patch, shares=shares, start=start),
-        out_shape=jax.ShapeDtypeStruct((kk * (patch // 2), LANES), F32),
-        in_specs=[vmem()], out_specs=vmem(),
-        compiler_params=pltpu.CompilerParams(vmem_limit_bytes=4 * 1024 * 1024),
-    )(psi)
-
-
-def list_kernel(list_ref, words_ref, amps_ref, piece_v, rank_v, *, patch, tile, taylor, origin):
+def list_components(list_ref, words_ref, amps_ref, piece_v, rank_v, *, patch, tile, taylor, origin):
     rows = tile + 2 * patch
     S = list_ref.shape[0] // LIST
 
@@ -200,27 +191,21 @@
         amps_ref[t * S:(t + 1) * S, :] = part[3 + 3 * t] + (part[4 + 3 * t] + part[5 + 3 * t])
 
 
-def overlapping(lists, origin, *, patch, tile, taylor):
-    S = lists.shape[0] // LIST
-    return pl.pallas_call(
-        functools.partial(list_kernel, patch=patch, tile=tile, taylor=taylor, origin=origin),
-        out_shape=(jax.ShapeDtypeStruct((S + 8, LANES), I32), jax.ShapeDtypeStruct((taylor * S, LANES), F32)),
-        in_specs=[vmem()], out_specs=(vmem(),) * 2,
-        scratch_shapes=[pltpu.VMEM(((3 + 3 * taylor) * S, LANES), F32), pltpu.VMEM((S, LANES), I32)],
-        compiler_params=pltpu.CompilerParams(vmem_limit_bytes=8 * 1024 * 1024),
-    )(lists)
-
-
-def render_kernel(words_ref, amps_ref, g_ref, gt_ref, dirty_hbm, res_ref, tay_ref,
-                  words_s, amps_s, dirty_ref, acc, acct, sems, *, patch, tile, taylor, scales):
+def render_kernel(list_ref, psi_ref, g_ref, dirty_hbm, res_ref, tay_ref,
+                  words_ref, amps_ref, piece_v, rank_v, gt_ref, words_s, amps_s, dirty_ref, acc, acct, sems, *,
+                  patch, tile, taylor, scales, origin, shares, start):
     rows = tile + 2 * patch
     S = words_ref.shape[0] - 8
     h = patch // 2
     copies = (pltpu.make_async_copy(words_ref, words_s, sems.at[0]),
               pltpu.make_async_copy(amps_ref, amps_s, sems.at[1]),
               pltpu.make_async_copy(dirty_hbm, dirty_ref, sems.at[2]))
-    for copy in copies:
-        copy.start()
+    copies[2].start()
+    list_components(list_ref, words_ref, amps_ref, piece_v, rank_v,
+                    patch=patch, tile=tile, taylor=taylor, origin=origin)
+    copies[0].start()
+    copies[1].start()
+    pack_fit(psi_ref, gt_ref, patch=patch, shares=shares, start=start)
     for j in range(1, acc.shape[0] // rows - 1):
         acc[pl.ds(j * rows + patch, tile), :] = jnp.zeros((tile, LANES), F32)
         acct[pl.ds(j * rows + patch - h, tile + h), :] = jnp.zeros((tile + h, LANES), F32)
@@ -273,19 +258,23 @@
         tay_ref[0, :, cols] = up + low
 
 
-def render(words, amps, g, gt, dirty, *, patch, taylor, scales):
-    tile = dirty.shape[1]
+def render(lists, psi, g, dirty, origin, start, *, patch, taylor, scales, shares):
+    tile, S = dirty.shape[1], lists.shape[0] // LIST
     rows, tiles = tile + 2 * patch, tile // HALF + 2
     return pl.pallas_call(
-        functools.partial(render_kernel, patch=patch, tile=tile, taylor=taylor, scales=scales),
+        functools.partial(render_kernel, patch=patch, tile=tile, taylor=taylor, scales=scales,
+                          origin=origin, shares=shares, start=start),
         out_shape=(jax.ShapeDtypeStruct(dirty.shape, F32), jax.ShapeDtypeStruct((1,) + dirty.shape[1:], F32)),
-        in_specs=[vmem()] * 4 + [pl.BlockSpec(memory_space=pltpu.HBM)], out_specs=(vmem(),) * 2,
+        in_specs=[vmem()] * 3 + [pl.BlockSpec(memory_space=pltpu.HBM)], out_specs=(vmem(),) * 2,
         scratch_shapes=[
-            pltpu.SMEM(words.shape, I32), pltpu.SMEM(amps.shape, F32), pltpu.VMEM(dirty.shape, F32),
+            pltpu.VMEM((S + 8, LANES), I32), pltpu.VMEM((taylor * S, LANES), F32),
+            pltpu.VMEM(((3 + 3 * taylor) * S, LANES), F32), pltpu.VMEM((S, LANES), I32),
+            pltpu.VMEM((g.shape[0] // 2, LANES), F32),
+            pltpu.SMEM((S + 8, LANES), I32), pltpu.SMEM((taylor * S, LANES), F32), pltpu.VMEM(dirty.shape, F32),
             pltpu.VMEM((tiles * rows, LANES), F32), pltpu.VMEM((tiles * rows, LANES), F32),
             pltpu.SemaphoreType.DMA((3,))],
-        compiler_params=pltpu.CompilerParams(vmem_limit_bytes=8 * 1024 * 1024),
-    )(words, amps, g, gt, pltpu.with_memory_space_constraint(dirty, pltpu.HBM))
+        compiler_params=pltpu.CompilerParams(vmem_limit_bytes=12 * 1024 * 1024),
+    )(lists, psi, g, pltpu.with_memory_space_constraint(dirty, pltpu.HBM))
 
 
 def finish_kernel(res_ref, total_ref, fit_ref, res_hbm, tay_hbm, tay_ref, sems):
@@ -347,15 +336,12 @@
     got = hop(jnp.concatenate([lists, psi[0]], 0), bits[-1])
     lists = jnp.concatenate([lists, got[:cut]], 0)
     psi = jnp.concatenate([psi[0], got[cut:]], 0)
-    words, amps = overlapping(
-        lists, lambda: (lax.axis_index("ty") * tile, lax.axis_index("tx") * tile),
-        patch=patch, tile=tile, taylor=taylor)
     for bit in band_bits:
         cut = total.shape[0] // 2
         total = total[:cut] + across(total[cut:] * lift, bit)
     residual, model_fit = render(
-        words, amps, g, pack_fit(psi, psf.shape[1], patch, shares, lambda s: share() ^ s), dirty,
-        patch=patch, taylor=taylor, scales=scales)
+        lists, psi, g, dirty, lambda: (lax.axis_index("ty") * tile, lax.axis_index("tx") * tile),
+        lambda s: share() ^ s, patch=patch, taylor=taylor, scales=scales, shares=shares)
     return finish(residual, total, model_fit)
 
 

time: 25.7 us -> 25.8 us (level)
  waiting for transfers between devices: 6.1 us -> 7.16 us
  Pallas kernels: 6.72 us -> 5.67 us
    ppermute x4, waiting for transfers between devices: 5.51 us -> 6.58 us  [across(): lax.ppermute(value.astype(jnp.float16), 'band', [(i, i ^ bit) for i in ra...]
    pallas_call x2 -> x0, Pallas kernels: 0.85 us -> none  [the longest x1 0.61 us: overlapping(): pl.pallas_call(functools.partial(list_kernel, patch=patch, tile=tile, tay...]
  transfers between devices with their start and end apart: 7 -> 7, of which waited for: 5 -> 5; matrix products, arithmetic and copies ran while one was open for 1% -> 1% of each run, Pallas kernels for 17% -> 13%
where the time goes in v2:
time: 25.8 us; the launch traced here: 25.6 us
  starting transfers between devices  11.7 us (45%)
  waiting for transfers between devices  7.16 us (28%)
  Pallas kernels  5.67 us (22%)
  between operations  0.72 us (3%)
  other arithmetic  0.28 us (1%)
    ppermute x4, starting transfers between devices, across(): lax.ppermute(value.astype(jnp.float16), 'band', [(i, i ^ bit) for i in ra...  8.62 us
    ppermute x4, waiting for transfers between devices, across(): lax.ppermute(value.astype(jnp.float16), 'band', [(i, i ^ bit) for i in ra...  6.58 us
    ppermute x3, starting transfers between devices, hop(): lax.ppermute(value, ('ty', 'tx'), [(i, i ^ bit) for i in range(n_ty * n_t...  3.08 us
    pallas_call x1, Pallas kernels, render(): pl.pallas_call(functools.partial(render_kernel, patch=patch, tile=tile, t...  2.99 us
    pallas_call x1, Pallas kernels, prep(): pl.pallas_call(functools.partial(prep_kernel, me=me, share=share, shares=...  1.41 us
    pallas_call x1, Pallas kernels, finish(): pl.pallas_call(finish_kernel, out_shape=(jax.ShapeDtypeStruct(residual.sh...  0.9 us
    ppermute x3, waiting for transfers between devices, hop(): lax.ppermute(value, ('ty', 'tx'), [(i, i ^ bit) for i in range(n_ty * n_t...  0.59 us
  transfers between devices with their start and end apart: 7, of which 5 were waited for; matrix products, arithmetic and copies ran while one was open for 1% of the time, Pallas kernels for 13%

profile of v2, /device:TPU:0, one launch (start us, length us, event | category | flops | bytes accessed | tf_op | source)
XLA Modules:
  0.0 25.6 jit_solution(7422558835568896096)
XLA Ops:
  0.6 1.4 %shard_map.86 = (f32[8,128]{1,0:T(8,128)S(1)}, f32[2,192,128]{2,1,0:T(8,128)S(1)}, f32[2,192,128]{2,1,0:T(8,128)S(1)}, f32[2,256,256]{2,1,0:T(8,128)S(1)}, f32[2...) custom-call(f32[2,4]{1,0:T(2,128)} %w_hbm.1, s32[1,128]{1,0:T(1,128)} %bitcast.10, s32[2,128]{1,0:T(2,128)} %bitcast.9, ...), custom_call_target="tpu_custom_call" | custom-call | tf_op jit(solution)/shard_map/pallas_call | solution.py:74
  2.1 3.1 %collective-permute-start.2 = (f16[2,192,128]{2,1,0:T(8,128)(2,1)S(1)}, f16[2,192,128]{2,1,0:T(8,128)(2,1)S(1)}, u32[]{:S(2)}, u32[]{:S(2)}) collective-permute-start(f16[2,192,128]{2,1,0:T(8,128)(2,1)S(1)} %convert_element_type.24), channel_id=1, source_target_pairs={{0,8},{8,0},{16,24},{24,16},{1,9},{9,1},{17,25},{25,17},{2,10},{10... | collective-permute-start | bytes 294920 | tf_op jit(solution)/shard_map/ppermute | solution.py:319
  5.2 1.5 %collective-permute-start = (f32[8,128]{1,0:T(8,128)S(1)}, f32[8,128]{1,0:T(8,128)S(1)}, u32[]{:S(2)}, u32[]{:S(2)}) collective-permute-start(f32[8,128]{1,0:T(8,128)S(1)} %get-tuple-element.10), channel_id=1, source_target_pairs={{0,1},{1,0},{2,3},{3,2},{4,5},{5,4},{6,7},{7,6},{8,9},{9,8},{10,11... | collective-permute-start | bytes 12296 | tf_op jit(solution)/shard_map/ppermute | solution.py:323
  6.7 0.5 %collective-permute-start.5 = (f16[2,256,256]{2,1,0:T(8,128)(2,1)S(1)}, f16[2,256,256]{2,1,0:T(8,128)(2,1)S(1)}, u32[]{:S(2)}, u32[]{:S(2)}) collective-permute-start(f16[2,256,256]{2,1,0:T(8,128)(2,1)S(1)} %convert_element_type.28), channel_id=1, source_target_pairs={{0,8},{8,0},{16,24},{24,16},{1,9},{9,1},{17,25},{25,17},{2,10},{10... | collective-permute-start | bytes 786440 | tf_op jit(solution)/shard_map/ppermute | solution.py:319
  7.2 0.4 %shard_map.87.g_ref = f32[960,128]{1,0:T(8,128)S(1)} custom-call(f32[720,128]{1,0:T(8,128)S(1)} %get-tuple-element.13.pairs_ref), custom_call_target="tpu_custom_call" | custom-call | tf_op jit(solution)/shard_map/pallas_call | solution.py:115
  7.6 0.5 %collective-permute-done.2 = f16[2,192,128]{2,1,0:T(8,128)(2,1)S(1)} collective-permute-done((f16[2,192,128]{2,1,0:T(8,128)(2,1)S(1)}, f16[2,192,128]{2,1,0:T(8,128)(2,1)S(1)}, u32[]{:S(2)}, u32[]{:S(2)}) %collective-permute-start.2) | collective-permute-done | bytes 98336 | tf_op jit(solution)/shard_map/ppermute | solution.py:319
  8.1 2.8 %collective-permute-start.3 = (f16[1,192,128]{2,1,0:T(8,128)(2,1)S(1)}, f16[1,192,128]{2,1,0:T(8,128)(2,1)S(1)}, u32[]{:S(2)}, u32[]{:S(2)}) collective-permute-start(f16[1,192,128]{2,1,0:T(8,128)(2,1)S(1)} %fusion.1), channel_id=1, source_target_pairs={{0,16},{8,24},{16,0},{24,8},{1,17},{9,25},{17,1},{25,9},{2,18},{10... | collective-permute-start | bytes 147464 | tf_op jit(solution)/shard_map/ppermute | solution.py:319
  10.9 0.0 collective-permute-done
  10.9 1.5 %collective-permute-start.1 = (f32[16,128]{1,0:T(8,128)S(1)}, f32[16,128]{1,0:T(8,128)S(1)}, u32[]{:S(2)}, u32[]{:S(2)}) collective-permute-start(f32[16,128]{1,0:T(8,128)S(1)} %pad_maximum_fusion.3), channel_id=1, source_target_pairs={{0,4},{1,5},{2,6},{3,7},{4,0},{5,1},{6,2},{7,3},{8,12},{9,13},{10,... | collective-permute-start | bytes 24584 | tf_op jit(solution)/shard_map/ppermute | solution.py:323
  12.4 1.5 %collective-permute-done.3 = f16[1,192,128]{2,1,0:T(8,128)(2,1)S(1)} collective-permute-done((f16[1,192,128]{2,1,0:T(8,128)(2,1)S(1)}, f16[1,192,128]{2,1,0:T(8,128)(2,1)S(1)}, u32[]{:S(2)}, u32[]{:S(2)}) %collective-permute-start.3) | collective-permute-done | bytes 49184 | tf_op jit(solution)/shard_map/ppermute | solution.py:319
  14.0 0.6 %collective-permute-done.1 = f32[16,128]{1,0:T(8,128)S(1)} collective-permute-done((f32[16,128]{1,0:T(8,128)S(1)}, f32[16,128]{1,0:T(8,128)S(1)}, u32[]{:S(2)}, u32[]{:S(2)}) %collective-permute-start.1) | collective-permute-done | bytes 8224 | tf_op jit(solution)/shard_map/ppermute | solution.py:323
  14.6 0.1 collective-permute-start.4
  14.7 0.6 %collective-permute-done.5 = f16[2,256,256]{2,1,0:T(8,128)(2,1)S(1)} collective-permute-done((f16[2,256,256]{2,1,0:T(8,128)(2,1)S(1)}, f16[2,256,256]{2,1,0:T(8,128)(2,1)S(1)}, u32[]{:S(2)}, u32[]{:S(2)}) %collective-permute-start.5) | collective-permute-done | bytes 262176 | tf_op jit(solution)/shard_map/ppermute | solution.py:319
  15.3 0.1 multiply_add_fusion
  15.4 2.3 %collective-permute-start.6 = (f16[1,256,256]{2,1,0:T(8,128)(2,1)S(1)}, f16[1,256,256]{2,1,0:T(8,128)(2,1)S(1)}, u32[]{:S(2)}, u32[]{:S(2)}) collective-permute-start(f16[1,256,256]{2,1,0:T(8,128)(2,1)S(1)} %fusion), channel_id=1, source_target_pairs={{0,16},{8,24},{16,0},{24,8},{1,17},{9,25},{17,1},{25,9},{2,18},{10... | collective-permute-start | bytes 393224 | tf_op jit(solution)/shard_map/ppermute | solution.py:319
  17.7 0.0 collective-permute-done.4
  17.7 3.0 %shard_map.88 = (f32[2,256,256]{2,1,0:T(8,128)S(1)}, f32[1,256,256]{2,1,0:T(8,128)S(1)}) custom-call(f32[64,128]{1,0:T(8,128)S(1)} %pad_maximum_fusion.2.list_ref, f32[384,128]{1,0:T(8,128)S(1)} %pad_maximum_fusion.psi_ref, f32[960,128]{1,0:T(8,128)S(1)} %shard_map.87.g_ref, f32[2,256,256]{2,1,0:T(8,128)} %dirty_hbm.3), custom_call_target="tpu_custom_call" | custom-call | tf_op jit(solution)/shard_map/pallas_call | solution.py:264
  20.7 3.9 %collective-permute-done.6 = f16[1,256,256]{2,1,0:T(8,128)(2,1)S(1)} collective-permute-done((f16[1,256,256]{2,1,0:T(8,128)(2,1)S(1)}, f16[1,256,256]{2,1,0:T(8,128)(2,1)S(1)}, u32[]{:S(2)}, u32[]{:S(2)}) %collective-permute-start.6) | collective-permute-done | bytes 131104 | tf_op jit(solution)/shard_map/ppermute | solution.py:319
  24.7 0.9 %shard_map.89 = (f32[2,256,256]{2,1,0:T(8,128)}, f32[1,256,256]{2,1,0:T(8,128)}) custom-call(f32[2,256,256]{2,1,0:T(8,128)S(1)} %get-tuple-element.14.res_ref, f32[1,256,256]{2,1,0:T(8,128)S(1)} %slice_add_fusion.total_ref, f32[1,256,256]{2,1,0:T(8,128)S(1)} %get-tuple-element.17.fit_ref), custom_call_target="tpu_custom_call" | custom-call | tf_op jit(solution)/shard_map/pallas_call | solution.py:291
  (13 shorter events, 0.2 us)
Async XLA Ops:
  2.1 6.0 %collective-permute-start.2 = (f16[2,192,128]{2,1,0:T(8,128)(2,1)S(1)}, f16[2,192,128]{2,1,0:T(8,128)(2,1)S(1)}, u32[]{:S(2)}, u32[]{:S(2)}) collective-permute-start(f16[2,192,128]{2,1,0:T(8,128)(2,1)S(1)} %convert_element_type.24), channel_id=1, source_target_pairs={{0,8},{8,0},{16,24},{24,16},{1,9},{9,1},{17,25},{25,17},{2,10},{10... | collective-permute-start | bytes 294920 | tf_op jit(solution)/shard_map/ppermute | solution.py:319
  5.2 5.8 %collective-permute-start = (f32[8,128]{1,0:T(8,128)S(1)}, f32[8,128]{1,0:T(8,128)S(1)}, u32[]{:S(2)}, u32[]{:S(2)}) collective-permute-start(f32[8,128]{1,0:T(8,128)S(1)} %get-tuple-element.10), channel_id=1, source_target_pairs={{0,1},{1,0},{2,3},{3,2},{4,5},{5,4},{6,7},{7,6},{8,9},{9,8},{10,11... | collective-permute-start | bytes 12296 | tf_op jit(solution)/shard_map/ppermute | solution.py:323
  6.7 8.6 %collective-permute-start.5 = (f16[2,256,256]{2,1,0:T(8,128)(2,1)S(1)}, f16[2,256,256]{2,1,0:T(8,128)(2,1)S(1)}, u32[]{:S(2)}, u32[]{:S(2)}) collective-permute-start(f16[2,256,256]{2,1,0:T(8,128)(2,1)S(1)} %convert_element_type.28), channel_id=1, source_target_pairs={{0,8},{8,0},{16,24},{24,16},{1,9},{9,1},{17,25},{25,17},{2,10},{10... | collective-permute-start | bytes 786440 | tf_op jit(solution)/shard_map/ppermute | solution.py:319
  8.1 5.8 %collective-permute-start.3 = (f16[1,192,128]{2,1,0:T(8,128)(2,1)S(1)}, f16[1,192,128]{2,1,0:T(8,128)(2,1)S(1)}, u32[]{:S(2)}, u32[]{:S(2)}) collective-permute-start(f16[1,192,128]{2,1,0:T(8,128)(2,1)S(1)} %fusion.1), channel_id=1, source_target_pairs={{0,16},{8,24},{16,0},{24,8},{1,17},{9,25},{17,1},{25,9},{2,18},{10... | collective-permute-start | bytes 147464 | tf_op jit(solution)/shard_map/ppermute | solution.py:319
  10.9 3.7 %collective-permute-start.1 = (f32[16,128]{1,0:T(8,128)S(1)}, f32[16,128]{1,0:T(8,128)S(1)}, u32[]{:S(2)}, u32[]{:S(2)}) collective-permute-start(f32[16,128]{1,0:T(8,128)S(1)} %pad_maximum_fusion.3), channel_id=1, source_target_pairs={{0,4},{1,5},{2,6},{3,7},{4,0},{5,1},{6,2},{7,3},{8,12},{9,13},{10,... | collective-permute-start | bytes 24584 | tf_op jit(solution)/shard_map/ppermute | solution.py:323
  14.6 3.1 %collective-permute-start.4 = (f32[224,128]{1,0:T(8,128)S(1)}, f32[224,128]{1,0:T(8,128)S(1)}, u32[]{:S(2)}, u32[]{:S(2)}) collective-permute-start(f32[224,128]{1,0:T(8,128)S(1)} %pad_maximum_fusion.1), channel_id=1, source_target_pairs={{0,2},{1,3},{2,0},{3,1},{4,6},{5,7},{6,4},{7,5},{8,10},{9,11},{10,... | collective-permute-start | bytes 344072 | tf_op jit(solution)/shard_map/ppermute | solution.py:323
  15.4 9.2 %collective-permute-start.6 = (f16[1,256,256]{2,1,0:T(8,128)(2,1)S(1)}, f16[1,256,256]{2,1,0:T(8,128)(2,1)S(1)}, u32[]{:S(2)}, u32[]{:S(2)}) collective-permute-start(f16[1,256,256]{2,1,0:T(8,128)(2,1)S(1)} %fusion), channel_id=1, source_target_pairs={{0,16},{8,24},{16,0},{24,8},{1,17},{9,25},{17,1},{25,9},{2,18},{10... | collective-permute-start | bytes 393224 | tf_op jit(solution)/shard_map/ppermute | solution.py:319

commit v3 on v2

--- a/solution.py
+++ b/solution.py
@@ -277,24 +277,20 @@
     )(lists, psi, g, pltpu.with_memory_space_constraint(dirty, pltpu.HBM))
 
 
-def finish_kernel(res_ref, total_ref, fit_ref, res_hbm, tay_hbm, tay_ref, sems):
-    res = pltpu.make_async_copy(res_ref, res_hbm, sems.at[0])
-    res.start()
-    tay_ref[...] = total_ref[...] - fit_ref[...]
-    tay = pltpu.make_async_copy(tay_ref, tay_hbm, sems.at[1])
-    tay.start()
-    res.wait()
-    tay.wait()
-
-
-def finish(residual, total, model_fit):
+def write_kernel(value_ref, out_hbm, sem):
+    copy = pltpu.make_async_copy(value_ref, out_hbm, sem)
+    copy.start()
+    copy.wait()
+
+
+def written(value):
     return pl.pallas_call(
-        finish_kernel,
-        out_shape=(jax.ShapeDtypeStruct(residual.shape, F32), jax.ShapeDtypeStruct(total.shape, F32)),
-        in_specs=[vmem()] * 3, out_specs=(pl.BlockSpec(memory_space=pltpu.HBM),) * 2,
-        scratch_shapes=[pltpu.VMEM(total.shape, F32), pltpu.SemaphoreType.DMA((2,))],
+        write_kernel,
+        out_shape=jax.ShapeDtypeStruct(value.shape, F32),
+        in_specs=[vmem()], out_specs=pl.BlockSpec(memory_space=pltpu.HBM),
+        scratch_shapes=[pltpu.SemaphoreType.DMA],
         compiler_params=pltpu.CompilerParams(vmem_limit_bytes=4 * 1024 * 1024),
-    )(residual, total, model_fit)
+    )(value)
 
 
 def per_device(dirty, psf, comp_tile, comp_offset, comp_scale, comp_amp, fit_weight):
@@ -342,7 +338,7 @@
     residual, model_fit = render(
         lists, psi, g, dirty, lambda: (lax.axis_index("ty") * tile, lax.axis_index("tx") * tile),
         lambda s: share() ^ s, patch=patch, taylor=taylor, scales=scales, shares=shares)
-    return finish(residual, total, model_fit)
+    return written(residual), total - model_fit
 
 
 def solution(mesh):

time: 25.8 us -> 25.7 us (level)
  waiting for transfers between devices: 7.16 us -> 6.07 us
  other arithmetic: 0.28 us -> 1 us
    ppermute x4, waiting for transfers between devices: 6.58 us -> 5.48 us  [across(): lax.ppermute(value.astype(jnp.float16), 'band', [(i, i ^ bit) for i in ra...]
    sub x0 -> x1, other arithmetic: none -> 0.75 us  [per_device(): return (written(residual), total - model_fit)]
    pallas_call x1, Pallas kernels: 2.99 us -> 3.28 us  [render(): pl.pallas_call(functools.partial(render_kernel, patch=patch, tile=tile, t...]
  transfers between devices with their start and end apart: 7 -> 7, of which waited for: 5 -> 5; matrix products, arithmetic and copies ran while one was open for 1% -> 1% of each run, Pallas kernels for 13% -> 18%
where the time goes in v3:
time: 25.7 us; the launch traced here: 25.4 us
  starting transfers between devices  11.7 us (46%)
  waiting for transfers between devices  6.07 us (24%)
  Pallas kernels  5.86 us (23%)
  other arithmetic  1 us (4%)
  between operations  0.73 us (3%)
    ppermute x4, starting transfers between devices, across(): lax.ppermute(value.astype(jnp.float16), 'band', [(i, i ^ bit) for i in ra...  8.62 us
    ppermute x4, waiting for transfers between devices, across(): lax.ppermute(value.astype(jnp.float16), 'band', [(i, i ^ bit) for i in ra...  5.48 us
    pallas_call x1, Pallas kernels, render(): pl.pallas_call(functools.partial(render_kernel, patch=patch, tile=tile, t...  3.28 us
    ppermute x3, starting transfers between devices, hop(): lax.ppermute(value, ('ty', 'tx'), [(i, i ^ bit) for i in range(n_ty * n_t...  3.08 us
    pallas_call x1, Pallas kernels, prep(): pl.pallas_call(functools.partial(prep_kernel, me=me, share=share, shares=...  1.41 us
    pallas_call x1, Pallas kernels, written(): pl.pallas_call(write_kernel, out_shape=jax.ShapeDtypeStruct(value.shape,...  0.8 us
    sub x1, other arithmetic, per_device(): return (written(residual), total - model_fit)  0.75 us
    ppermute x3, waiting for transfers between devices, hop(): lax.ppermute(value, ('ty', 'tx'), [(i, i ^ bit) for i in range(n_ty * n_t...  0.59 us
  transfers between devices with their start and end apart: 7, of which 5 were waited for; matrix products, arithmetic and copies ran while one was open for 1% of the time, Pallas kernels for 18%

profile of v3, /device:TPU:0, one launch (start us, length us, event | category | flops | bytes accessed | tf_op | source)
XLA Modules:
  0.0 25.4 jit_solution(6242740848500980809)
XLA Ops:
  0.6 1.4 %shard_map.86 = (f32[8,128]{1,0:T(8,128)S(1)}, f32[2,192,128]{2,1,0:T(8,128)S(1)}, f32[2,192,128]{2,1,0:T(8,128)S(1)}, f32[2,256,256]{2,1,0:T(8,128)S(1)}, f32[2...) custom-call(f32[2,4]{1,0:T(2,128)} %w_hbm.1, s32[1,128]{1,0:T(1,128)} %bitcast.10, s32[2,128]{1,0:T(2,128)} %bitcast.9, ...), custom_call_target="tpu_custom_call" | custom-call | tf_op jit(solution)/shard_map/pallas_call | solution.py:74
  2.1 3.1 %collective-permute-start.2 = (f16[2,192,128]{2,1,0:T(8,128)(2,1)S(1)}, f16[2,192,128]{2,1,0:T(8,128)(2,1)S(1)}, u32[]{:S(2)}, u32[]{:S(2)}) collective-permute-start(f16[2,192,128]{2,1,0:T(8,128)(2,1)S(1)} %convert_element_type.24), channel_id=1, source_target_pairs={{0,8},{8,0},{16,24},{24,16},{1,9},{9,1},{17,25},{25,17},{2,10},{10... | collective-permute-start | bytes 294920 | tf_op jit(solution)/shard_map/ppermute | solution.py:315
  5.2 1.5 %collective-permute-start = (f32[8,128]{1,0:T(8,128)S(1)}, f32[8,128]{1,0:T(8,128)S(1)}, u32[]{:S(2)}, u32[]{:S(2)}) collective-permute-start(f32[8,128]{1,0:T(8,128)S(1)} %get-tuple-element.10), channel_id=1, source_target_pairs={{0,1},{1,0},{2,3},{3,2},{4,5},{5,4},{6,7},{7,6},{8,9},{9,8},{10,11... | collective-permute-start | bytes 12296 | tf_op jit(solution)/shard_map/ppermute | solution.py:319
  6.7 0.5 %collective-permute-start.5 = (f16[2,256,256]{2,1,0:T(8,128)(2,1)S(1)}, f16[2,256,256]{2,1,0:T(8,128)(2,1)S(1)}, u32[]{:S(2)}, u32[]{:S(2)}) collective-permute-start(f16[2,256,256]{2,1,0:T(8,128)(2,1)S(1)} %convert_element_type.28), channel_id=1, source_target_pairs={{0,8},{8,0},{16,24},{24,16},{1,9},{9,1},{17,25},{25,17},{2,10},{10... | collective-permute-start | bytes 786440 | tf_op jit(solution)/shard_map/ppermute | solution.py:315
  7.2 0.4 %shard_map.87.g_ref = f32[960,128]{1,0:T(8,128)S(1)} custom-call(f32[720,128]{1,0:T(8,128)S(1)} %get-tuple-element.13.pairs_ref), custom_call_target="tpu_custom_call" | custom-call | tf_op jit(solution)/shard_map/pallas_call | solution.py:115
  7.6 0.5 %collective-permute-done.2 = f16[2,192,128]{2,1,0:T(8,128)(2,1)S(1)} collective-permute-done((f16[2,192,128]{2,1,0:T(8,128)(2,1)S(1)}, f16[2,192,128]{2,1,0:T(8,128)(2,1)S(1)}, u32[]{:S(2)}, u32[]{:S(2)}) %collective-permute-start.2) | collective-permute-done | bytes 98336 | tf_op jit(solution)/shard_map/ppermute | solution.py:315
  8.1 2.8 %collective-permute-start.3 = (f16[1,192,128]{2,1,0:T(8,128)(2,1)S(1)}, f16[1,192,128]{2,1,0:T(8,128)(2,1)S(1)}, u32[]{:S(2)}, u32[]{:S(2)}) collective-permute-start(f16[1,192,128]{2,1,0:T(8,128)(2,1)S(1)} %fusion.2), channel_id=1, source_target_pairs={{0,16},{8,24},{16,0},{24,8},{1,17},{9,25},{17,1},{25,9},{2,18},{10... | collective-permute-start | bytes 147464 | tf_op jit(solution)/shard_map/ppermute | solution.py:315
  10.9 0.0 collective-permute-done
  10.9 1.5 %collective-permute-start.1 = (f32[16,128]{1,0:T(8,128)S(1)}, f32[16,128]{1,0:T(8,128)S(1)}, u32[]{:S(2)}, u32[]{:S(2)}) collective-permute-start(f32[16,128]{1,0:T(8,128)S(1)} %pad_maximum_fusion.3), channel_id=1, source_target_pairs={{0,4},{1,5},{2,6},{3,7},{4,0},{5,1},{6,2},{7,3},{8,12},{9,13},{10,... | collective-permute-start | bytes 24584 | tf_op jit(solution)/shard_map/ppermute | solution.py:319
  12.4 1.5 %collective-permute-done.3 = f16[1,192,128]{2,1,0:T(8,128)(2,1)S(1)} collective-permute-done((f16[1,192,128]{2,1,0:T(8,128)(2,1)S(1)}, f16[1,192,128]{2,1,0:T(8,128)(2,1)S(1)}, u32[]{:S(2)}, u32[]{:S(2)}) %collective-permute-start.3) | collective-permute-done | bytes 49184 | tf_op jit(solution)/shard_map/ppermute | solution.py:315
  14.0 0.6 %collective-permute-done.1 = f32[16,128]{1,0:T(8,128)S(1)} collective-permute-done((f32[16,128]{1,0:T(8,128)S(1)}, f32[16,128]{1,0:T(8,128)S(1)}, u32[]{:S(2)}, u32[]{:S(2)}) %collective-permute-start.1) | collective-permute-done | bytes 8224 | tf_op jit(solution)/shard_map/ppermute | solution.py:319
  14.6 0.1 collective-permute-start.4
  14.7 0.6 %collective-permute-done.5 = f16[2,256,256]{2,1,0:T(8,128)(2,1)S(1)} collective-permute-done((f16[2,256,256]{2,1,0:T(8,128)(2,1)S(1)}, f16[2,256,256]{2,1,0:T(8,128)(2,1)S(1)}, u32[]{:S(2)}, u32[]{:S(2)}) %collective-permute-start.5) | collective-permute-done | bytes 262176 | tf_op jit(solution)/shard_map/ppermute | solution.py:315
  15.3 0.1 multiply_add_fusion
  15.4 2.3 %collective-permute-start.6 = (f16[1,256,256]{2,1,0:T(8,128)(2,1)S(1)}, f16[1,256,256]{2,1,0:T(8,128)(2,1)S(1)}, u32[]{:S(2)}, u32[]{:S(2)}) collective-permute-start(f16[1,256,256]{2,1,0:T(8,128)(2,1)S(1)} %fusion), channel_id=1, source_target_pairs={{0,16},{8,24},{16,0},{24,8},{1,17},{9,25},{17,1},{25,9},{2,18},{10... | collective-permute-start | bytes 393224 | tf_op jit(solution)/shard_map/ppermute | solution.py:315
  17.7 0.0 collective-permute-done.4
  17.7 3.3 %shard_map.88 = (f32[2,256,256]{2,1,0:T(8,128)S(1)}, f32[1,256,256]{2,1,0:T(8,128)S(1)}) custom-call(f32[64,128]{1,0:T(8,128)S(1)} %pad_maximum_fusion.2.list_ref, f32[384,128]{1,0:T(8,128)S(1)} %pad_maximum_fusion.psi_ref, f32[960,128]{1,0:T(8,128)S(1)} %shard_map.87.g_ref, f32[2,256,256]{2,1,0:T(8,128)} %dirty_hbm.3), custom_call_target="tpu_custom_call" | custom-call | tf_op jit(solution)/shard_map/pallas_call | solution.py:264
  21.0 0.8 %shard_map.89 = f32[2,256,256]{2,1,0:T(8,128)} custom-call(f32[2,256,256]{2,1,0:T(8,128)S(1)} %get-tuple-element.14.value_ref), custom_call_target="tpu_custom_call" | custom-call | tf_op jit(solution)/shard_map/pallas_call | solution.py:287
  21.8 2.8 %collective-permute-done.6 = f16[1,256,256]{2,1,0:T(8,128)(2,1)S(1)} collective-permute-done((f16[1,256,256]{2,1,0:T(8,128)(2,1)S(1)}, f16[1,256,256]{2,1,0:T(8,128)(2,1)S(1)}, u32[]{:S(2)}, u32[]{:S(2)}) %collective-permute-start.6) | collective-permute-done | bytes 131104 | tf_op jit(solution)/shard_map/ppermute | solution.py:315
  24.6 0.7 %fusion.1 = f32[1,256,256]{2,1,0:T(8,128)} fusion(f32[1,256,256]{2,1,0:T(8,128)S(1)} %get-tuple-element.17, f32[2,256,256]{2,1,0:T(8,128)S(1)} %multiply_add_fusion, f16[1,256,256]{2,1,0:T(8,128)(2,1)S(1)} %collective-permute-done.6), kind=kLoop, calls=%fused_computation.4 | loop fusion | flops 262144 | bytes 917504 | tf_op jit(solution)/shard_map/sub | solution.py:341
  (12 shorter events, 0.2 us)
Async XLA Ops:
  2.1 6.0 %collective-permute-start.2 = (f16[2,192,128]{2,1,0:T(8,128)(2,1)S(1)}, f16[2,192,128]{2,1,0:T(8,128)(2,1)S(1)}, u32[]{:S(2)}, u32[]{:S(2)}) collective-permute-start(f16[2,192,128]{2,1,0:T(8,128)(2,1)S(1)} %convert_element_type.24), channel_id=1, source_target_pairs={{0,8},{8,0},{16,24},{24,16},{1,9},{9,1},{17,25},{25,17},{2,10},{10... | collective-permute-start | bytes 294920 | tf_op jit(solution)/shard_map/ppermute | solution.py:315
  5.2 5.8 %collective-permute-start = (f32[8,128]{1,0:T(8,128)S(1)}, f32[8,128]{1,0:T(8,128)S(1)}, u32[]{:S(2)}, u32[]{:S(2)}) collective-permute-start(f32[8,128]{1,0:T(8,128)S(1)} %get-tuple-element.10), channel_id=1, source_target_pairs={{0,1},{1,0},{2,3},{3,2},{4,5},{5,4},{6,7},{7,6},{8,9},{9,8},{10,11... | collective-permute-start | bytes 12296 | tf_op jit(solution)/shard_map/ppermute | solution.py:319
  6.7 8.6 %collective-permute-start.5 = (f16[2,256,256]{2,1,0:T(8,128)(2,1)S(1)}, f16[2,256,256]{2,1,0:T(8,128)(2,1)S(1)}, u32[]{:S(2)}, u32[]{:S(2)}) collective-permute-start(f16[2,256,256]{2,1,0:T(8,128)(2,1)S(1)} %convert_element_type.28), channel_id=1, source_target_pairs={{0,8},{8,0},{16,24},{24,16},{1,9},{9,1},{17,25},{25,17},{2,10},{10... | collective-permute-start | bytes 786440 | tf_op jit(solution)/shard_map/ppermute | solution.py:315
  8.1 5.8 %collective-permute-start.3 = (f16[1,192,128]{2,1,0:T(8,128)(2,1)S(1)}, f16[1,192,128]{2,1,0:T(8,128)(2,1)S(1)}, u32[]{:S(2)}, u32[]{:S(2)}) collective-permute-start(f16[1,192,128]{2,1,0:T(8,128)(2,1)S(1)} %fusion.2), channel_id=1, source_target_pairs={{0,16},{8,24},{16,0},{24,8},{1,17},{9,25},{17,1},{25,9},{2,18},{10... | collective-permute-start | bytes 147464 | tf_op jit(solution)/shard_map/ppermute | solution.py:315
  10.9 3.7 %collective-permute-start.1 = (f32[16,128]{1,0:T(8,128)S(1)}, f32[16,128]{1,0:T(8,128)S(1)}, u32[]{:S(2)}, u32[]{:S(2)}) collective-permute-start(f32[16,128]{1,0:T(8,128)S(1)} %pad_maximum_fusion.3), channel_id=1, source_target_pairs={{0,4},{1,5},{2,6},{3,7},{4,0},{5,1},{6,2},{7,3},{8,12},{9,13},{10,... | collective-permute-start | bytes 24584 | tf_op jit(solution)/shard_map/ppermute | solution.py:319
  14.6 3.1 %collective-permute-start.4 = (f32[224,128]{1,0:T(8,128)S(1)}, f32[224,128]{1,0:T(8,128)S(1)}, u32[]{:S(2)}, u32[]{:S(2)}) collective-permute-start(f32[224,128]{1,0:T(8,128)S(1)} %pad_maximum_fusion.1), channel_id=1, source_target_pairs={{0,2},{1,3},{2,0},{3,1},{4,6},{5,7},{6,4},{7,5},{8,10},{9,11},{10,... | collective-permute-start | bytes 344072 | tf_op jit(solution)/shard_map/ppermute | solution.py:319
  15.4 9.2 %collective-permute-start.6 = (f16[1,256,256]{2,1,0:T(8,128)(2,1)S(1)}, f16[1,256,256]{2,1,0:T(8,128)(2,1)S(1)}, u32[]{:S(2)}, u32[]{:S(2)}) collective-permute-start(f16[1,256,256]{2,1,0:T(8,128)(2,1)S(1)} %fusion), channel_id=1, source_target_pairs={{0,16},{8,24},{16,0},{24,8},{1,17},{9,25},{17,1},{25,9},{2,18},{10... | collective-permute-start | bytes 393224 | tf_op jit(solution)/shard_map/ppermute | solution.py:315

commit v4 on v2

--- a/solution.py
+++ b/solution.py
@@ -191,6 +191,12 @@
         amps_ref[t * S:(t + 1) * S, :] = part[3 + 3 * t] + (part[4 + 3 * t] + part[5 + 3 * t])
 
 
+def pairwise(terms):
+    while len(terms) > 1:
+        terms = [sum(terms[n + 1:n + 2], terms[n]) for n in range(0, len(terms), 2)]
+    return terms[0]
+
+
 def render_kernel(list_ref, psi_ref, g_ref, dirty_hbm, res_ref, tay_ref,
                   words_ref, amps_ref, piece_v, rank_v, gt_ref, words_s, amps_s, dirty_ref, acc, acct, sems, *,
                   patch, tile, taylor, scales, origin, shares, start):
@@ -219,12 +225,12 @@
         word = words_s[row, col]
         base, turn, width = word & 16383, (word >> 14) & (LANES - 1), word >> 21
         gb, hb = pl.multiple_of(width * patch, 8), pl.multiple_of(width * h, 8)
-        p = q = None
+        ps, qs = [], []
         for t in range(taylor):
             a = amps_s[row + t * S, col]
-            x = a * g_ref[pl.ds(gb + t * scales * patch, patch), :]
-            y = a * gt_ref[pl.ds(hb + t * scales * h, h), :]
-            p, q = (x, y) if p is None else (p + x, q + y)
+            ps.append(a * g_ref[pl.ds(gb + t * scales * patch, patch), :])
+            qs.append(a * gt_ref[pl.ds(hb + t * scales * h, h), :])
+        p, q = pairwise(ps), pairwise(qs)
         p = p.astype(BF16).astype(F32)
         return pltpu.roll(p, turn, 1), pltpu.roll(q, turn, 1), base, turn & (HALF - 1)
 
@@ -278,12 +284,15 @@
 
 
 def finish_kernel(res_ref, total_ref, fit_ref, res_hbm, tay_hbm, tay_ref, sems):
-    res = pltpu.make_async_copy(res_ref, res_hbm, sems.at[0])
-    res.start()
+    bands = res_ref.shape[0]
+    res = [pltpu.make_async_copy(res_ref.at[b], res_hbm.at[b], sems.at[1 + b]) for b in range(bands)]
+    for copy in res:
+        copy.start()
     tay_ref[...] = total_ref[...] - fit_ref[...]
-    tay = pltpu.make_async_copy(tay_ref, tay_hbm, sems.at[1])
+    tay = pltpu.make_async_copy(tay_ref, tay_hbm, sems.at[0])
     tay.start()
-    res.wait()
+    for copy in res:
+        copy.wait()
     tay.wait()
 
 
@@ -292,7 +301,7 @@
         finish_kernel,
         out_shape=(jax.ShapeDtypeStruct(residual.shape, F32), jax.ShapeDtypeStruct(total.shape, F32)),
         in_specs=[vmem()] * 3, out_specs=(pl.BlockSpec(memory_space=pltpu.HBM),) * 2,
-        scratch_shapes=[pltpu.VMEM(total.shape, F32), pltpu.SemaphoreType.DMA((2,))],
+        scratch_shapes=[pltpu.VMEM(total.shape, F32), pltpu.SemaphoreType.DMA((1 + residual.shape[0],))],
         compiler_params=pltpu.CompilerParams(vmem_limit_bytes=4 * 1024 * 1024),
     )(residual, total, model_fit)
 

time: 25.8 us -> 25.9 us (level)
  Pallas kernels: 5.67 us -> 6.8 us
  waiting for transfers between devices: 7.16 us -> 6.04 us
    pallas_call x1, Pallas kernels: 2.99 us -> 4.12 us  [render(): pl.pallas_call(functools.partial(render_kernel, patch=patch, tile=tile, t...]
    ppermute x4, waiting for transfers between devices: 6.58 us -> 5.45 us  [across(): lax.ppermute(value.astype(jnp.float16), 'band', [(i, i ^ bit) for i in ra...]
  transfers between devices with their start and end apart: 7 -> 7, of which waited for: 5 -> 5; matrix products, arithmetic and copies ran while one was open for 1% -> 1% of each run, Pallas kernels for 13% -> 18%
where the time goes in v4:
time: 25.9 us; the launch traced here: 25.6 us
  starting transfers between devices  11.7 us (45%)
  Pallas kernels  6.8 us (26%)
  waiting for transfers between devices  6.04 us (23%)
  between operations  0.72 us (3%)
  other arithmetic  0.28 us (1%)
    ppermute x4, starting transfers between devices, across(): lax.ppermute(value.astype(jnp.float16), 'band', [(i, i ^ bit) for i in ra...  8.62 us
    ppermute x4, waiting for transfers between devices, across(): lax.ppermute(value.astype(jnp.float16), 'band', [(i, i ^ bit) for i in ra...  5.45 us
    pallas_call x1, Pallas kernels, render(): pl.pallas_call(functools.partial(render_kernel, patch=patch, tile=tile, t...  4.12 us
    ppermute x3, starting transfers between devices, hop(): lax.ppermute(value, ('ty', 'tx'), [(i, i ^ bit) for i in range(n_ty * n_t...  3.08 us
    pallas_call x1, Pallas kernels, prep(): pl.pallas_call(functools.partial(prep_kernel, me=me, share=share, shares=...  1.41 us
    pallas_call x1, Pallas kernels, finish(): pl.pallas_call(finish_kernel, out_shape=(jax.ShapeDtypeStruct(residual.sh...  0.9 us
    ppermute x3, waiting for transfers between devices, hop(): lax.ppermute(value, ('ty', 'tx'), [(i, i ^ bit) for i in range(n_ty * n_t...  0.59 us
  transfers between devices with their start and end apart: 7, of which 5 were waited for; matrix products, arithmetic and copies ran while one was open for 1% of the time, Pallas kernels for 18%

profile of v4, /device:TPU:0, one launch (start us, length us, event | category | flops | bytes accessed | tf_op | source)
XLA Modules:
  0.0 25.6 jit_solution(12819555391472301970)
XLA Ops:
  0.6 1.4 %shard_map.86 = (f32[8,128]{1,0:T(8,128)S(1)}, f32[2,192,128]{2,1,0:T(8,128)S(1)}, f32[2,192,128]{2,1,0:T(8,128)S(1)}, f32[2,256,256]{2,1,0:T(8,128)S(1)}, f32[2...) custom-call(f32[2,4]{1,0:T(2,128)} %w_hbm.1, s32[1,128]{1,0:T(1,128)} %bitcast.10, s32[2,128]{1,0:T(2,128)} %bitcast.9, ...), custom_call_target="tpu_custom_call" | custom-call | tf_op jit(solution)/shard_map/pallas_call | solution.py:74
  2.1 3.1 %collective-permute-start.2 = (f16[2,192,128]{2,1,0:T(8,128)(2,1)S(1)}, f16[2,192,128]{2,1,0:T(8,128)(2,1)S(1)}, u32[]{:S(2)}, u32[]{:S(2)}) collective-permute-start(f16[2,192,128]{2,1,0:T(8,128)(2,1)S(1)} %convert_element_type.24), channel_id=1, source_target_pairs={{0,8},{8,0},{16,24},{24,16},{1,9},{9,1},{17,25},{25,17},{2,10},{10... | collective-permute-start | bytes 294920 | tf_op jit(solution)/shard_map/ppermute | solution.py:328
  5.2 1.5 %collective-permute-start = (f32[8,128]{1,0:T(8,128)S(1)}, f32[8,128]{1,0:T(8,128)S(1)}, u32[]{:S(2)}, u32[]{:S(2)}) collective-permute-start(f32[8,128]{1,0:T(8,128)S(1)} %get-tuple-element.10), channel_id=1, source_target_pairs={{0,1},{1,0},{2,3},{3,2},{4,5},{5,4},{6,7},{7,6},{8,9},{9,8},{10,11... | collective-permute-start | bytes 12296 | tf_op jit(solution)/shard_map/ppermute | solution.py:332
  6.7 0.5 %collective-permute-start.5 = (f16[2,256,256]{2,1,0:T(8,128)(2,1)S(1)}, f16[2,256,256]{2,1,0:T(8,128)(2,1)S(1)}, u32[]{:S(2)}, u32[]{:S(2)}) collective-permute-start(f16[2,256,256]{2,1,0:T(8,128)(2,1)S(1)} %convert_element_type.28), channel_id=1, source_target_pairs={{0,8},{8,0},{16,24},{24,16},{1,9},{9,1},{17,25},{25,17},{2,10},{10... | collective-permute-start | bytes 786440 | tf_op jit(solution)/shard_map/ppermute | solution.py:328
  7.2 0.4 %shard_map.87.g_ref = f32[960,128]{1,0:T(8,128)S(1)} custom-call(f32[720,128]{1,0:T(8,128)S(1)} %get-tuple-element.13.pairs_ref), custom_call_target="tpu_custom_call" | custom-call | tf_op jit(solution)/shard_map/pallas_call | solution.py:115
  7.6 0.5 %collective-permute-done.2 = f16[2,192,128]{2,1,0:T(8,128)(2,1)S(1)} collective-permute-done((f16[2,192,128]{2,1,0:T(8,128)(2,1)S(1)}, f16[2,192,128]{2,1,0:T(8,128)(2,1)S(1)}, u32[]{:S(2)}, u32[]{:S(2)}) %collective-permute-start.2) | collective-permute-done | bytes 98336 | tf_op jit(solution)/shard_map/ppermute | solution.py:328
  8.1 2.8 %collective-permute-start.3 = (f16[1,192,128]{2,1,0:T(8,128)(2,1)S(1)}, f16[1,192,128]{2,1,0:T(8,128)(2,1)S(1)}, u32[]{:S(2)}, u32[]{:S(2)}) collective-permute-start(f16[1,192,128]{2,1,0:T(8,128)(2,1)S(1)} %fusion.1), channel_id=1, source_target_pairs={{0,16},{8,24},{16,0},{24,8},{1,17},{9,25},{17,1},{25,9},{2,18},{10... | collective-permute-start | bytes 147464 | tf_op jit(solution)/shard_map/ppermute | solution.py:328
  10.9 0.0 collective-permute-done
  10.9 1.5 %collective-permute-start.1 = (f32[16,128]{1,0:T(8,128)S(1)}, f32[16,128]{1,0:T(8,128)S(1)}, u32[]{:S(2)}, u32[]{:S(2)}) collective-permute-start(f32[16,128]{1,0:T(8,128)S(1)} %pad_maximum_fusion.3), channel_id=1, source_target_pairs={{0,4},{1,5},{2,6},{3,7},{4,0},{5,1},{6,2},{7,3},{8,12},{9,13},{10,... | collective-permute-start | bytes 24584 | tf_op jit(solution)/shard_map/ppermute | solution.py:332
  12.4 1.5 %collective-permute-done.3 = f16[1,192,128]{2,1,0:T(8,128)(2,1)S(1)} collective-permute-done((f16[1,192,128]{2,1,0:T(8,128)(2,1)S(1)}, f16[1,192,128]{2,1,0:T(8,128)(2,1)S(1)}, u32[]{:S(2)}, u32[]{:S(2)}) %collective-permute-start.3) | collective-permute-done | bytes 49184 | tf_op jit(solution)/shard_map/ppermute | solution.py:328
  14.0 0.6 %collective-permute-done.1 = f32[16,128]{1,0:T(8,128)S(1)} collective-permute-done((f32[16,128]{1,0:T(8,128)S(1)}, f32[16,128]{1,0:T(8,128)S(1)}, u32[]{:S(2)}, u32[]{:S(2)}) %collective-permute-start.1) | collective-permute-done | bytes 8224 | tf_op jit(solution)/shard_map/ppermute | solution.py:332
  14.6 0.1 collective-permute-start.4
  14.7 0.6 %collective-permute-done.5 = f16[2,256,256]{2,1,0:T(8,128)(2,1)S(1)} collective-permute-done((f16[2,256,256]{2,1,0:T(8,128)(2,1)S(1)}, f16[2,256,256]{2,1,0:T(8,128)(2,1)S(1)}, u32[]{:S(2)}, u32[]{:S(2)}) %collective-permute-start.5) | collective-permute-done | bytes 262176 | tf_op jit(solution)/shard_map/ppermute | solution.py:328
  15.3 0.1 multiply_add_fusion
  15.4 2.3 %collective-permute-start.6 = (f16[1,256,256]{2,1,0:T(8,128)(2,1)S(1)}, f16[1,256,256]{2,1,0:T(8,128)(2,1)S(1)}, u32[]{:S(2)}, u32[]{:S(2)}) collective-permute-start(f16[1,256,256]{2,1,0:T(8,128)(2,1)S(1)} %fusion), channel_id=1, source_target_pairs={{0,16},{8,24},{16,0},{24,8},{1,17},{9,25},{17,1},{25,9},{2,18},{10... | collective-permute-start | bytes 393224 | tf_op jit(solution)/shard_map/ppermute | solution.py:328
  17.7 0.0 collective-permute-done.4
  17.7 4.1 %shard_map.88 = (f32[2,256,256]{2,1,0:T(8,128)S(1)}, f32[1,256,256]{2,1,0:T(8,128)S(1)}) custom-call(f32[64,128]{1,0:T(8,128)S(1)} %pad_maximum_fusion.2.list_ref, f32[384,128]{1,0:T(8,128)S(1)} %pad_maximum_fusion.psi_ref, f32[960,128]{1,0:T(8,128)S(1)} %shard_map.87.g_ref, f32[2,256,256]{2,1,0:T(8,128)} %dirty_hbm.3), custom_call_target="tpu_custom_call" | custom-call | tf_op jit(solution)/shard_map/pallas_call | solution.py:270
  21.8 2.8 %collective-permute-done.6 = f16[1,256,256]{2,1,0:T(8,128)(2,1)S(1)} collective-permute-done((f16[1,256,256]{2,1,0:T(8,128)(2,1)S(1)}, f16[1,256,256]{2,1,0:T(8,128)(2,1)S(1)}, u32[]{:S(2)}, u32[]{:S(2)}) %collective-permute-start.6) | collective-permute-done | bytes 131104 | tf_op jit(solution)/shard_map/ppermute | solution.py:328
  24.7 0.9 %shard_map.89 = (f32[2,256,256]{2,1,0:T(8,128)}, f32[1,256,256]{2,1,0:T(8,128)}) custom-call(f32[2,256,256]{2,1,0:T(8,128)S(1)} %get-tuple-element.14.res_ref, f32[1,256,256]{2,1,0:T(8,128)S(1)} %slice_add_fusion.total_ref, f32[1,256,256]{2,1,0:T(8,128)S(1)} %get-tuple-element.17.fit_ref), custom_call_target="tpu_custom_call" | custom-call | tf_op jit(solution)/shard_map/pallas_call | solution.py:300
  (13 shorter events, 0.2 us)
Async XLA Ops:
  2.1 6.0 %collective-permute-start.2 = (f16[2,192,128]{2,1,0:T(8,128)(2,1)S(1)}, f16[2,192,128]{2,1,0:T(8,128)(2,1)S(1)}, u32[]{:S(2)}, u32[]{:S(2)}) collective-permute-start(f16[2,192,128]{2,1,0:T(8,128)(2,1)S(1)} %convert_element_type.24), channel_id=1, source_target_pairs={{0,8},{8,0},{16,24},{24,16},{1,9},{9,1},{17,25},{25,17},{2,10},{10... | collective-permute-start | bytes 294920 | tf_op jit(solution)/shard_map/ppermute | solution.py:328
  5.2 5.8 %collective-permute-start = (f32[8,128]{1,0:T(8,128)S(1)}, f32[8,128]{1,0:T(8,128)S(1)}, u32[]{:S(2)}, u32[]{:S(2)}) collective-permute-start(f32[8,128]{1,0:T(8,128)S(1)} %get-tuple-element.10), channel_id=1, source_target_pairs={{0,1},{1,0},{2,3},{3,2},{4,5},{5,4},{6,7},{7,6},{8,9},{9,8},{10,11... | collective-permute-start | bytes 12296 | tf_op jit(solution)/shard_map/ppermute | solution.py:332
  6.7 8.6 %collective-permute-start.5 = (f16[2,256,256]{2,1,0:T(8,128)(2,1)S(1)}, f16[2,256,256]{2,1,0:T(8,128)(2,1)S(1)}, u32[]{:S(2)}, u32[]{:S(2)}) collective-permute-start(f16[2,256,256]{2,1,0:T(8,128)(2,1)S(1)} %convert_element_type.28), channel_id=1, source_target_pairs={{0,8},{8,0},{16,24},{24,16},{1,9},{9,1},{17,25},{25,17},{2,10},{10... | collective-permute-start | bytes 786440 | tf_op jit(solution)/shard_map/ppermute | solution.py:328
  8.1 5.8 %collective-permute-start.3 = (f16[1,192,128]{2,1,0:T(8,128)(2,1)S(1)}, f16[1,192,128]{2,1,0:T(8,128)(2,1)S(1)}, u32[]{:S(2)}, u32[]{:S(2)}) collective-permute-start(f16[1,192,128]{2,1,0:T(8,128)(2,1)S(1)} %fusion.1), channel_id=1, source_target_pairs={{0,16},{8,24},{16,0},{24,8},{1,17},{9,25},{17,1},{25,9},{2,18},{10... | collective-permute-start | bytes 147464 | tf_op jit(solution)/shard_map/ppermute | solution.py:328
  10.9 3.7 %collective-permute-start.1 = (f32[16,128]{1,0:T(8,128)S(1)}, f32[16,128]{1,0:T(8,128)S(1)}, u32[]{:S(2)}, u32[]{:S(2)}) collective-permute-start(f32[16,128]{1,0:T(8,128)S(1)} %pad_maximum_fusion.3), channel_id=1, source_target_pairs={{0,4},{1,5},{2,6},{3,7},{4,0},{5,1},{6,2},{7,3},{8,12},{9,13},{10,... | collective-permute-start | bytes 24584 | tf_op jit(solution)/shard_map/ppermute | solution.py:332
  14.6 3.1 %collective-permute-start.4 = (f32[224,128]{1,0:T(8,128)S(1)}, f32[224,128]{1,0:T(8,128)S(1)}, u32[]{:S(2)}, u32[]{:S(2)}) collective-permute-start(f32[224,128]{1,0:T(8,128)S(1)} %pad_maximum_fusion.1), channel_id=1, source_target_pairs={{0,2},{1,3},{2,0},{3,1},{4,6},{5,7},{6,4},{7,5},{8,10},{9,11},{10,... | collective-permute-start | bytes 344072 | tf_op jit(solution)/shard_map/ppermute | solution.py:332
  15.4 9.2 %collective-permute-start.6 = (f16[1,256,256]{2,1,0:T(8,128)(2,1)S(1)}, f16[1,256,256]{2,1,0:T(8,128)(2,1)S(1)}, u32[]{:S(2)}, u32[]{:S(2)}) collective-permute-start(f16[1,256,256]{2,1,0:T(8,128)(2,1)S(1)} %fusion), channel_id=1, source_target_pairs={{0,16},{8,24},{16,0},{24,8},{1,17},{9,25},{17,1},{25,9},{2,18},{10... | collective-permute-start | bytes 393224 | tf_op jit(solution)/shard_map/ppermute | solution.py:328
